TPU v7x, 128 devices: a whole 4x4x4 slice. The times are simulated.
128 devices in a mesh: seq: 32 (over z, x, y_lo), dp: 4 (over y_hi, core).
Axes of the slice: x: 4, y: 4 (y_hi: 2, y_lo: 2; y = y_hi * 2 + y_lo), z: 4, core: 2. Of those that a mesh axis runs over, the one named last changes fastest.
Arguments:
- inputs: bfloat16 [4, 1024, 64, 1024], P('dp', 'seq'), may hold values from -6 to 6
- gate_in: bfloat16 [4, 1024, 64, 1024], P('dp', 'seq'), may hold values from -6 to 6
- cotangent: bfloat16 [4, 1024, 64, 1024], P('dp', 'seq'), may hold values from -6 to 6
- right_factor: bfloat16 [1024, 1024], replicated, may hold values from -0.1875 to 0.1875
- left_factor: bfloat16 [1024, 1024], replicated, may hold values from -0.1875 to 0.1875
- mask_tiles: int32 [8, 8], replicated, may hold values from 0 to 1, as said below
Outputs:
- grad_input: bfloat16 [4, 1024, 64, 1024], P('dp', 'seq')
- grad_gate: bfloat16 [4, 1024, 64, 1024], P('dp', 'seq')
- grad_right: float32 [1024, 1024], P(('seq', 'dp'))
- grad_left: float32 [1024, 1024], P(('seq', 'dp'))
Inputs may be any that keep to these rules, and one draw needn't show every extreme that they name: `mask_tiles`: 1 on every diagonal tile, 0 above the diagonal, 0 or 1 below it.
All inputs are finite; a program needn't handle non-finite values.
Results may differ from a plain program's by a relative error of at most 0.0058.
Values may be sent and summed in bfloat16 or wider, within the bound.
No kernel may reach another device: no remote copies, remote signals or barrier semaphores. Data moves between devices by JAX's collectives and lax.ppermute only.
A program may use at most 192 MiB of HBM per device.

v0:
```python
import math

import jax
import jax.numpy as jnp
from jax import lax
from jax.sharding import PartitionSpec as P


def expand_mask(mask_tiles, size):
    tiles = mask_tiles.shape[0]
    side = size // tiles
    values = mask_tiles.astype(jnp.float32)
    return jnp.broadcast_to(values[:, None, :, None], (tiles, side, tiles, side)).reshape(
        size, size
    )


def reduce_factor(term, width, seq_count, data_count):
    return lax.psum_scatter(
        term(jnp.int32(0), width // (seq_count * data_count) * lax.axis_size(("seq", "dp"))),
        ("seq", "dp"),
        scatter_dimension=0,
        tiled=True,
    )


def shards(inputs, gate_in, cotangent, right_factor, left_factor, mask_tiles):
    width = right_factor.shape[0]
    channels = inputs.shape[2]
    own_blocks = inputs.shape[1]
    seq_count = lax.axis_size("seq")
    data_count = lax.axis_size("dp")
    full_mask = expand_mask(mask_tiles, width)
    right_masked = (right_factor.astype(jnp.float32) * full_mask).astype(jnp.bfloat16)
    left_masked = (left_factor.astype(jnp.float32) * full_mask).astype(jnp.bfloat16)
    signal = inputs[0]
    first_section = jnp.einsum(
        "icj,kj->ick", signal, right_masked, preferred_element_type=jnp.float32
    ).astype(jnp.bfloat16)
    columns = lax.all_to_all(first_section, "seq", split_axis=1, concat_axis=0, tiled=True)
    mixed = jnp.einsum(
        "ui,ick->uck", left_masked, columns, preferred_element_type=jnp.float32
    ).astype(jnp.bfloat16)
    mixed_rows = lax.all_to_all(mixed, "seq", split_axis=0, concat_axis=1, tiled=True)
    sig = jax.nn.sigmoid(gate_in[0].astype(jnp.float32))
    cot_f = cotangent[0].astype(jnp.float32)
    grad_gate = (cot_f * mixed_rows.astype(jnp.float32) * sig * (1.0 - sig)).astype(jnp.bfloat16)
    grad_rows = (cot_f * sig).astype(jnp.bfloat16)
    grad_piece = lax.all_to_all(grad_rows, "seq", split_axis=1, concat_axis=0, tiled=True)
    inner_cols = jnp.einsum(
        "ui,uck->ick", left_masked, grad_piece, preferred_element_type=jnp.float32
    ).astype(jnp.bfloat16)
    flat_width = grad_piece.shape[1] * grad_piece.shape[2]
    first_flat = columns.reshape(width, flat_width)

    def left_term(start, count):
        rows_piece = grad_piece.reshape(count, flat_width)
        return lax.dot_general(
            rows_piece, first_flat, (((1,), (1,)), ((), ())), preferred_element_type=jnp.float32
        )

    left_sum = reduce_factor(left_term, width, seq_count, data_count)
    inner_split = inner_cols.reshape(seq_count, own_blocks, inner_cols.shape[1], width)
    inner_piece = lax.all_to_all(inner_split, "seq", split_axis=0, concat_axis=2, tiled=True)
    back = jnp.einsum(
        "aick,kj->aicj", inner_piece, right_masked, preferred_element_type=jnp.float32
    ).astype(jnp.bfloat16)
    inner_rows = inner_piece
    inner_rows = inner_rows[0]

    def right_term(start, count):
        return jnp.einsum("ick,icj->kj", inner_rows, signal, preferred_element_type=jnp.float32)

    right_sum = reduce_factor(right_term, width, seq_count, data_count)
    own_rows = width // (seq_count * data_count)
    owner = (lax.axis_index("seq") * data_count + lax.axis_index("dp")) * own_rows
    mask_rows = lax.dynamic_slice_in_dim(full_mask, owner, own_rows, 0)
    scale = 1.0 / math.sqrt(data_count * channels * width)
    grad_left = left_sum * mask_rows * scale
    grad_right = right_sum * mask_rows * scale
    return (back, grad_gate[None], grad_right, grad_left)


def solution(mesh):
    placed = (
        P("dp", "seq", None, None),
        P("dp", "seq", None, None),
        P("dp", "seq", None, None),
        P(),
        P(),
        P(),
    )
    return jax.shard_map(
        shards,
        mesh=mesh,
        in_specs=placed,
        out_specs=(
            P("dp", "seq", None, None),
            P("dp", "seq", None, None),
            P(("seq", "dp"), None),
            P(("seq", "dp"), None),
        ),
        check_vma=False,
    )
```

profile of v0, /device:TPU:0, one launch (start us, length us, event | category | flops | bytes accessed | tf_op | source)
XLA Modules:
  0.0 1552.5 jit_solution(16793548192921058287)
XLA Ops:
  7.2 0.0 copy-start.11
  7.2 0.8 convert_element_type.74
  8.0 0.3 broadcast_in_dim.2
  8.4 0.0 copy-start.2
  8.4 1.2 copy-done.11
  9.5 6.9 convert_bitcast_fusion
  16.5 0.0 copy-done.2
  16.5 2.3 copy.29
  18.8 60.9 %all_to_all.60 = bf16[32,64,1024]{2,0,1:T(8,128)(2,1)} all-to-all(bf16[32,64,1024]{2,0,1:T(8,128)(2,1)S(1)} %copy.29), channel_id=1, replica_groups=mesh['seq'=32,'dp'=4] {'seq'}, dimensions={1} | all-to-all | bytes 8388608 | tf_op jit(solution)/shard_map/all_to_all | solution.py:40
  79.7 6.5 copy.70
  86.2 0.0 copy-start
  86.2 0.0 copy-start.3
  86.2 0.0 copy-start.13
  86.2 1.4 copy.31
  87.6 1.0 copy-done
  88.7 1.3 copy-done.3
  89.9 0.7 copy-done.13
  90.6 6.4 convolution_convert_fusion
  97.0 6.5 copy.32
  103.5 55.6 %all_to_all.61 = bf16[1024,2,1024]{2,1,0:T(2,128)(2,1)S(1)} all-to-all(bf16[1024,2,1024]{2,1,0:T(2,128)(2,1)S(1)} %copy.32), channel_id=1, replica_groups=mesh['seq'=32,'dp'=4] {'seq'}, dimensions={0} | all-to-all | bytes 8388608 | tf_op jit(solution)/shard_map/all_to_all | solution.py:44
  159.0 0.0 copy-start.9
  159.0 0.0 copy-start.10
  159.0 1.5 copy.33
  160.6 0.6 copy-done.9
  161.2 1.3 copy-done.10
  162.5 16.8 %fusion.3 = (bf16[1,32,64,1024]{3,1,2,0:T(8,128)(2,1)}, bf16[32,64,1024]{2,0,1:T(8,128)(2,1)}) fusion(bf16[1,32,64,1024]{3,2,1,0:T(8,128)(2,1)S(1)} %copy-done.9, bf16[1,32,64,1024]{3,2,1,0:T(8,128)(2,1)S(1)} %copy-done.10, f32[1,32,64,1024]{3,1,2,0:T(8,128)S(1)} %bitcast.74), kind=kLoop, calls=%fused_computation.5 | loop fusion | flops 25165824 | bytes 25165824 | tf_op jit(solution)/shard_map/convert_element_type | solution.py:47
  179.3 4.9 all-to-all-start
  184.2 0.5 reduce-scatter.5.cloned.1.call-start
  184.7 5.5 copy.40
  190.2 48.5 %all-to-all-done = bf16[32,64,1024]{2,0,1:T(8,128)(2,1)} async-done(((bf16[32,64,1024]{2,0,1:T(8,128)(2,1)}), bf16[32,64,1024]{2,0,1:T(8,128)(2,1)}, u32[]{:S(2)}, u32[]{:S(2)}) %all-to-all-start) | async-done | bytes 4194336 | tf_op jit(solution)/shard_map/all_to_all | solution.py:49
  238.7 6.5 copy.71
  245.3 0.0 copy-start.1
  245.3 0.0 copy-start.8
  245.3 1.5 copy.39
  246.8 1.0 copy-done.1
  247.8 1.2 copy-done.8
  249.0 6.1 fusion.29
  255.1 0.0 reduce-scatter.5.cloned.1.call-update
  255.1 0.2 reduce-scatter.3.cloned.1.call-start
  255.3 0.0 copy-start.4
  255.3 3.7 copy.25
  259.1 0.0 copy-done.4
  259.1 5.8 convolution_convert_fusion.1
  264.9 0.5 copy.27
  265.5 0.0 copy-start.12
  265.5 54.1 %all_to_all.62 = bf16[32,32,2,1024]{3,1,2,0:T(8,128)(2,1)S(1)} all-to-all(bf16[32,32,2,1024]{3,1,2,0:T(8,128)(2,1)S(1)} %copy.27), channel_id=1, replica_groups=mesh['seq'=32,'dp'=4] {'seq'}, dimensions={0} | all-to-all | bytes 8388608 | tf_op jit(solution)/shard_map/all_to_all | solution.py:64
  319.6 0.0 copy-start.6
  319.6 1.9 copy-done.6
  321.6 0.0 copy-done.12
  321.6 6.4 fusion.16
  327.9 0.0 reduce-scatter.3.cloned.1.call-update
  328.0 0.0 copy-start.14
  328.0 5.3 copy.69
  333.3 0.0 copy-start.5
  333.3 0.0 copy-start.7
  333.3 6.7 copy.34
  340.0 0.0 copy-done.14
  340.0 0.0 copy-done.5
  340.0 0.0 copy-done.7
  340.0 8.2 convert_bitcast_fusion.1
  348.2 556.7 %reduce-scatter.5.cloned.1.call-done = f32[8,1024]{1,0:T(8,128)} async-done(((f32[1024,1024]{1,0:T(8,128)}), f32[8,1024]{1,0:T(8,128)}) %reduce-scatter.5.cloned.1.call-update) | async-done | bytes 32784 | tf_op jit(solution)/shard_map/reduce_scatter | solution.py:19
  904.9 639.1 %reduce-scatter.3.cloned.1.call-done = f32[8,1024]{1,0:T(8,128)} async-done(((f32[1024,1024]{1,0:T(8,128)}), f32[8,1024]{1,0:T(8,128)}) %reduce-scatter.3.cloned.1.call-update) | async-done | bytes 32784 | tf_op jit(solution)/shard_map/reduce_scatter | solution.py:19
  1544.0 1.4 multiply_multiply_fusion
Async XLA Ops:
  7.2 2.4 copy-start.11
  8.4 8.1 copy-start.2
  86.2 2.4 copy-start
  86.2 3.7 copy-start.3
  86.2 4.4 copy-start.13
  159.0 2.2 copy-start.9
  159.0 3.5 copy-start.10
  179.3 59.4 %all-to-all-start = ((bf16[32,64,1024]{2,0,1:T(8,128)(2,1)}), bf16[32,64,1024]{2,0,1:T(8,128)(2,1)}, u32[]{:S(2)}, u32[]{:S(2)}) async-start(bf16[32,64,1024]{2,0,1:T(8,128)(2,1)} %get-tuple-element.9), calls=%async_computation | async-start | bytes 8388608 | tf_op jit(solution)/shard_map/all_to_all | solution.py:49
  184.2 720.7 %reduce-scatter.5.cloned.1.call-start = ((), (), s32[]{:S(2)}) async-start(), calls=%async_computation.7 | async-start | bytes 4227072 | tf_op jit(solution)/shard_map/reduce_scatter | solution.py:19
  245.3 2.5 copy-start.1
  245.3 3.7 copy-start.8
  255.1 1288.9 %reduce-scatter.3.cloned.1.call-start = ((), (), s32[]{:S(2)}) async-start(), calls=%async_computation.6 | async-start | bytes 4227072 | tf_op jit(solution)/shard_map/reduce_scatter | solution.py:19
  255.3 3.7 copy-start.4
  265.5 56.1 %copy-start.12 = (bf16[1,32,64,1024]{3,2,1,0:T(8,128)(2,1)S(1)}, bf16[1,32,64,1024]{3,2,1,0:T(8,128)(2,1)}, u32[]{:S(2)}) copy-start(bf16[1,32,64,1024]{3,2,1,0:T(8,128)(2,1)} %param.6) | copy-start | bytes 12582916
  319.6 1.9 copy-start.6
  328.0 12.0 copy-start.14
  333.3 6.7 copy-start.5
  333.3 6.7 copy-start.7
Sparse Core Ops, SparseCore 0:
  255.2 649.6 reduce-scatter.4
  907.4 636.5 reduce-scatter.2
where the time goes:
time: 1560 us; the launch traced here: 1550 us
  waiting for transfers between devices  1240 us (79%)
  blocking collectives  171 us (11%)
  local copies, waits for them, and re-layouts  58.6 us (4%)
  matrix products  39.8 us (3%)
  other arithmetic  19.1 us (1%)
    reduce_scatter x2, waiting for transfers between devices, reduce_factor(): lax.psum_scatter(term(jnp.int32(0), width // (seq_count * data_count) * l...  1200 us
    all_to_all x1, blocking collectives, shards(): lax.all_to_all(first_section, 'seq', split_axis=1, concat_axis=0, tiled=T...  60.9 us
    all_to_all x1, blocking collectives, shards(): lax.all_to_all(mixed, 'seq', split_axis=0, concat_axis=1, tiled=True)  55.6 us
    all_to_all x1, blocking collectives, shards(): lax.all_to_all(inner_split, 'seq', split_axis=0, concat_axis=2, tiled=True)  54.1 us
    all_to_all x1, waiting for transfers between devices, shards(): lax.all_to_all(grad_rows, 'seq', split_axis=1, concat_axis=0, tiled=True)  48.5 us
  transfers between devices with their start and end apart: 3, of which 3 were waited for; matrix products, arithmetic and copies ran while one was open for 3% of the time, Pallas kernels for 0%

commit v1 on v0

v1 whole, which is shorter than its diff:
```python
import math

import jax
import jax.numpy as jnp
from jax import lax
from jax.experimental import pallas as pl
from jax.experimental.pallas import tpu as pltpu
from jax.sharding import PartitionSpec as P

BF = jnp.bfloat16
F32 = jnp.float32
MIB = 1024 * 1024
SUB = 16
SIDE = 256


def params(mib):
    return pltpu.CompilerParams(vmem_limit_bytes=mib * MIB)


def shape(dims, dtype):
    return jax.ShapeDtypeStruct(dims, dtype)


def dot(a, b, on_a, on_b):
    return lax.dot_general(a, b, (((on_a,), (on_b,)), ((), ())), preferred_element_type=F32)


def turn(values):
    size = SUB * SUB
    row = lax.broadcasted_iota(jnp.int32, (size, size), 0)
    col = lax.broadcasted_iota(jnp.int32, (size, size), 1)
    other = row % SUB * SUB + row // SUB
    matrix = jnp.where(col == other, 1.0, 0.0).astype(BF)
    return dot(matrix, values, 1, 0)


def spread_kernel(x_ref, cot_ref, gate_ref, out_ref):
    size, width = SUB * SUB, x_ref.shape[3]
    dims = (SUB // 2, 2, SUB, width)
    out_ref[:, :, 0] = turn(x_ref[0].reshape(size, width)).astype(BF).reshape(dims)
    sig = jax.nn.sigmoid(gate_ref[0].astype(F32))
    grad = (cot_ref[0].astype(F32) * sig).astype(BF)
    out_ref[:, :, 1] = turn(grad.reshape(size, width)).astype(BF).reshape(dims)


def gather_kernel(in_ref, cot_ref, gate_ref, back_ref, grad_ref):
    size, width = SUB * SUB, cot_ref.shape[3]
    dims = (SUB, SUB, width)
    back_ref[0] = turn(in_ref[:, :, 1].reshape(size, width)).astype(BF).reshape(dims)
    mixed = turn(in_ref[:, :, 0].reshape(size, width)).reshape(dims)
    sig = jax.nn.sigmoid(gate_ref[0].astype(F32))
    cot = cot_ref[0].astype(F32)
    grad_ref[0] = (cot * mixed * sig * (1.0 - sig)).astype(BF)


def retile_specs(dims):
    _, rows, channels, width = dims
    natural = pl.BlockSpec((1, SUB, SUB, width), lambda i, c: (0, i, c, 0))
    apart = pl.BlockSpec((SUB // 2, 2, 2, SUB, width), lambda i, c: (c, 0, 0, i, 0))
    return (rows // SUB, channels // SUB), natural, apart


def spread(x, cot, gate):
    _, rows, channels, width = x.shape
    grid, natural, apart = retile_specs(x.shape)
    return pl.pallas_call(
        spread_kernel,
        grid=grid,
        in_specs=[natural] * 3,
        out_specs=apart,
        out_shape=shape((channels // 2, 2, 2, rows, width), BF),
        compiler_params=params(40),
    )(x, cot, gate)


def gather(parts, cot, gate):
    grid, natural, apart = retile_specs(cot.shape)
    return pl.pallas_call(
        gather_kernel,
        grid=grid,
        in_specs=[apart, natural, natural],
        out_specs=(natural, natural),
        out_shape=(shape(cot.shape, BF), shape(cot.shape, BF)),
        compiler_params=params(40),
    )(parts, cot, gate)


def mask_factor(tiles_ref, in_ref, out_ref):
    count = tiles_ref.shape[0]
    side = in_ref.shape[0] // count
    for a in range(count):
        rows = slice(a * side, (a + 1) * side)
        for b in range(count):
            cols = slice(b * side, (b + 1) * side)
            if b > a:
                out_ref[rows, cols] = jnp.zeros((side, side), BF)
            else:
                value = tiles_ref[a, b].astype(F32)
                out_ref[rows, cols] = (in_ref[rows, cols].astype(F32) * value).astype(BF)


def mix_kernel(
    at_ref, tiles_ref, left_ref, right_ref, in_ref,
    out_ref, own_ref, give1_ref, give2_ref, give3_ref,
    left, right, first, grad_first, sum_l, sum_r,
):
    step = pl.program_id(0)

    @pl.when(step == 0)
    def _():
        mask_factor(tiles_ref, left_ref, left)
        mask_factor(tiles_ref, right_ref, right)
        sum_l[...] = jnp.zeros_like(sum_l)
        sum_r[...] = jnp.zeros_like(sum_r)

    width = left.shape[0]
    devices, rows = in_ref.shape[0], in_ref.shape[3]
    blocks = [(at, at + SIDE) for at in range(0, width, SIDE)]
    x = in_ref[:, 0, 0].reshape(width, width)
    g = in_ref[:, 0, 1].reshape(width, width)

    def by_device(part):
        return part.reshape(part.shape[0] // rows, rows, part.shape[1])

    for at, end in blocks:
        first[:, at:end] = dot(x[:, :end], right[at:end, :end], 1, 1).astype(BF)
    for at, end in blocks:
        part = dot(left[at:end, :end], first[:end], 1, 0).astype(BF)
        out_ref[at // rows : end // rows, 0, 0] = by_device(part)
    for at, end in blocks:
        grad_first[at:end] = dot(left[at:, at:end], g[at:], 0, 0).astype(BF)
    for at, end in blocks:
        part = dot(grad_first[:, at:], right[at:, at:end], 1, 0).astype(BF)
        out_ref[:, 0, 1, :, at:end] = by_device(part)

    def add(total, at, end, part):
        inner = total.shape[1:3]
        count = SIDE // (inner[0] * inner[1])
        begin = at // (inner[0] * inner[1])
        total[begin : begin + count, :, :, :end] += part.reshape(count, *inner, end)

    for at, end in blocks:
        add(sum_l, at, end, dot(g[at:end], first[:end], 1, 1))
        add(sum_r, at, end, dot(grad_first[:, at:end], x[:, :end], 0, 0))

    @pl.when(step == 1)
    def _():
        for k, ref in enumerate((own_ref, give1_ref, give2_ref, give3_ref)):
            quarter = at_ref[0] ^ k
            both = (sum_l[:, quarter], sum_r[:, quarter])
            ref[...] = jnp.concatenate(both, axis=1).astype(ref.dtype)


def mix(at, tiles, left, right, parts, own):
    devices, _, _, rows, width = parts.shape
    channel = pl.BlockSpec((devices, 1, 2, rows, width), lambda c: (0, c, 0, 0, 0))
    factor = pl.BlockSpec((width, width), lambda c: (0, 0), pipeline_mode=pl.Buffered(1))
    quarter = pl.BlockSpec((devices, 2 * own, width), lambda c: (0, 0, 0))
    smem = pl.BlockSpec(memory_space=pltpu.SMEM)
    square = pltpu.VMEM((width, width), BF)
    total = pltpu.VMEM((devices, rows // own, own, width), F32)
    dims = (devices, 2 * own, width)
    return pl.pallas_call(
        mix_kernel,
        grid=(2,),
        in_specs=[smem, smem, factor, factor, channel],
        out_specs=(channel,) + (quarter,) * 4,
        out_shape=(shape(parts.shape, BF), shape(dims, F32)) + (shape(dims, BF),) * 3,
        scratch_shapes=[square, square, square, square, total, total],
        compiler_params=params(62),
    )(at, tiles, left, right, parts)


def swap(x):
    return lax.all_to_all(x, "seq", split_axis=0, concat_axis=0, tiled=True)


def shards(inputs, gate_in, cotangent, right_factor, left_factor, mask_tiles):
    width = right_factor.shape[0]
    channels = inputs.shape[2]
    seq_count = lax.axis_size("seq")
    data_count = lax.axis_size("dp")
    own = width // (seq_count * data_count)
    seq_at, data_at = lax.axis_index("seq"), lax.axis_index("dp")

    parts = swap(spread(inputs, cotangent, gate_in))
    at = jnp.full((1,), data_at, jnp.int32)
    parts, total, *give = mix(at, mask_tiles, left_factor, right_factor, parts, own)

    got = []
    for k in range(1, data_count):
        pairs = [
            (s * data_count + d, (s ^ (k // 2)) * data_count + (d ^ k))
            for s in range(seq_count)
            for d in range(data_count)
        ]
        got.append(lax.ppermute(give[k - 1], ("seq", "dp"), pairs))
    parts = swap(parts)
    total, parts = lax.optimization_barrier((total, parts))
    for other in got:
        total = total + other.astype(F32)
    total = swap(total.astype(BF))
    grad_input, grad_gate = gather(parts, cotangent, gate_in)

    sums = jnp.sum(total.astype(F32), 0)
    owner = (seq_at * data_count + data_at) * own
    scale = 1.0 / math.sqrt(data_count * channels * width)
    side = width // mask_tiles.shape[0]
    mask_row = lax.dynamic_slice_in_dim(mask_tiles, owner // side, 1, 0).astype(F32)
    mask_row = jnp.repeat(mask_row, side, axis=1) * scale
    return (grad_input, grad_gate, sums[own:] * mask_row, sums[:own] * mask_row)


def solution(mesh):
    placed = (
        P("dp", "seq", None, None),
        P("dp", "seq", None, None),
        P("dp", "seq", None, None),
        P(),
        P(),
        P(),
    )
    return jax.shard_map(
        shards,
        mesh=mesh,
        in_specs=placed,
        out_specs=(
            P("dp", "seq", None, None),
            P("dp", "seq", None, None),
            P(("seq", "dp"), None),
            P(("seq", "dp"), None),
        ),
        check_vma=False,
    )
```

time: 1560 us -> 326 us (0.21)
  waiting for transfers between devices: 1240 us -> 223 us
  blocking collectives: 171 us -> 0 us
  local copies, waits for them, and re-layouts: 58.6 us -> 11 us
  Pallas kernels: 0 us -> 43.3 us
  matrix products: 39.8 us -> 0 us
  starting transfers between devices: 5.58 us -> 42.5 us
    reduce_scatter x2 -> x0, waiting for transfers between devices: 1200 us -> none  [reduce_factor(): lax.psum_scatter(term(jnp.int32(0), width // (seq_count * data_count) * l...]
    all_to_all x1 -> x3, waiting for transfers between devices: 48.5 us -> 223 us  [swap(): return lax.all_to_all(x, 'seq', split_axis=0, concat_axis=0, tiled=True)]
    all_to_all x3 -> x0, blocking collectives: 171 us -> none  [the longest x1 60.9 us: shards(): lax.all_to_all(first_section, 'seq', split_axis=1, concat_axis=0, tiled=T...]
    pallas_call x0 -> x3, Pallas kernels: none -> 43.3 us  [the longest x1 26 us: mix(): pl.pallas_call(mix_kernel, grid=(2,), in_specs=[smem, smem, factor, facto...]
    dot_general x6 -> x0, matrix products: 39.8 us -> none  [the longest x1 8.21 us: shards(): jnp.einsum('aick,kj->aicj', inner_piece, right_masked, preferred_element_...]
    all_to_all x1 -> x3, starting transfers between devices: 4.86 us -> 39.2 us  [swap(): return lax.all_to_all(x, 'seq', split_axis=0, concat_axis=0, tiled=True)]
    unnamed x34 -> x12, local copies, waits for them, and re-layouts: 29.3 us -> 10.9 us
    all_to_all x4 -> x0, local copies, waits for them, and re-layouts: 18.1 us -> none  [the longest x2 10.2 us: shards(): lax.all_to_all(grad_rows, 'seq', split_axis=1, concat_axis=0, tiled=True)]
  transfers between devices with their start and end apart: 3 -> 6, of which waited for: 3 -> 3; matrix products, arithmetic and copies ran while one was open for 3% -> 0% of each run, Pallas kernels for 0% -> 3%
where the time goes in v1:
time: 326 us; the launch traced here: 325 us
  waiting for transfers between devices  223 us (68%)
  Pallas kernels  43.3 us (13%)
  starting transfers between devices  42.5 us (13%)
  local copies, waits for them, and re-layouts  11 us (3%)
  other arithmetic  4.84 us (1%)
    all_to_all x3, waiting for transfers between devices, swap(): return lax.all_to_all(x, 'seq', split_axis=0, concat_axis=0, tiled=True)  223 us
    all_to_all x3, starting transfers between devices, swap(): return lax.all_to_all(x, 'seq', split_axis=0, concat_axis=0, tiled=True)  39.2 us
    pallas_call x1, Pallas kernels, mix(): pl.pallas_call(mix_kernel, grid=(2,), in_specs=[smem, smem, factor, facto...  26 us
    unnamed x12, local copies, waits for them, and re-layouts  10.9 us
    pallas_call x1, Pallas kernels, gather(): pl.pallas_call(gather_kernel, grid=grid, in_specs=[apart, natural, natura...  10.2 us
    pallas_call x1, Pallas kernels, spread(): pl.pallas_call(spread_kernel, grid=grid, in_specs=[natural] * 3, out_spec...  7.07 us
  transfers between devices with their start and end apart: 6, of which 3 were waited for; matrix products, arithmetic and copies ran while one was open for 0% of the time, Pallas kernels for 3%

profile of v1, /device:TPU:0, one launch (start us, length us, event | category | flops | bytes accessed | tf_op | source)
XLA Modules:
  0.0 325.0 jit_solution(9137064408978600866)
XLA Ops:
  0.6 0.0 copy-start
  0.6 2.2 copy-done
  2.8 0.0 copy-start.2
  2.8 2.2 copy-done.2
  5.0 0.0 copy-start.4
  5.0 2.2 copy-done.4
  7.2 7.1 %shard_map.93 = bf16[32,2,2,32,1024]{4,3,2,1,0:T(8,128)(2,1)} custom-call(bf16[1,32,64,1024]{3,2,1,0:T(8,128)(2,1)S(1)} %copy-done.4, bf16[1,32,64,1024]{3,2,1,0:T(8,128)(2,1)S(1)} %copy-done, bf16[1,32,64,1024]{3,2,1,0:T(8,128)(2,1)S(1)} %copy-done.2), custom_call_target="tpu_custom_call" | custom-call | tf_op jit(solution)/shard_map/pallas_call | solution.py:67
  14.3 9.4 %all-to-all-start = ((bf16[32,2,2,32,1024]{4,3,2,1,0:T(8,128)(2,1)}), bf16[32,2,2,32,1024]{4,3,2,1,0:T(8,128)(2,1)}, u32[]{:S(2)}, u32[]{:S(2)}) async-start(bf16[32,2,2,32,1024]{4,3,2,1,0:T(8,128)(2,1)} %shard_map.93), calls=%async_computation | async-start | bytes 16777216 | tf_op jit(solution)/shard_map/all_to_all | solution.py:176
  23.7 120.7 %all-to-all-done.in_ref = bf16[32,2,2,32,1024]{4,3,2,1,0:T(8,128)(2,1)} async-done(((bf16[32,2,2,32,1024]{4,3,2,1,0:T(8,128)(2,1)}), bf16[32,2,2,32,1024]{4,3,2,1,0:T(8,128)(2,1)}, u32[]{:S(2)}, u32[]{:S(2)}) %all-to-all-start) | async-done | bytes 8388640 | tf_op jit(solution)/shard_map/all_to_all | solution.py:176
  144.4 26.0 %shard_map.94 = (bf16[32,2,2,32,1024]{4,3,2,1,0:T(8,128)(2,1)}, f32[32,16,1024]{2,1,0:T(8,128)}, bf16[32,16,1024]{2,1,0:T(8,128)(2,1)}, bf16[32,16,1024]{2,1,0:T(8,128)(2,1)}, bf16[32,16,1024]{2,1,0:T(8,128)(2,1)}) custom-call(s32[1]{0:T(128)} %bitcast.at_ref, s32[8,8]{1,0:T(8,128)} %tiles_ref.1, bf16[1024,1024]{1,0:T(8,128)(2,1)} %left_ref.1, ...), custom_call_target="tpu_custom_call" | custom-call | tf_op jit(solution)/shard_map/pallas_call | solution.py:164
  170.4 0.0 copy-start.5
  170.4 11.0 %all-to-all-start.1 = ((bf16[32,2,2,32,1024]{4,3,2,1,0:T(8,128)(2,1)}), bf16[32,2,2,32,1024]{4,3,2,1,0:T(8,128)(2,1)}, u32[]{:S(2)}, u32[]{:S(2)}) async-start(bf16[32,2,2,32,1024]{4,3,2,1,0:T(8,128)(2,1)} %get-tuple-element.14), calls=%async_computation.1 | async-start | bytes 16777216 | tf_op jit(solution)/shard_map/all_to_all | solution.py:176
  181.4 0.8 collective-permute-start.2
  182.2 2.4 collective-permute-start.1
  184.6 0.0 collective-permute-start
  184.7 101.8 %all-to-all-done.1.in_ref = bf16[32,2,2,32,1024]{4,3,2,1,0:T(8,128)(2,1)} async-done(((bf16[32,2,2,32,1024]{4,3,2,1,0:T(8,128)(2,1)}), bf16[32,2,2,32,1024]{4,3,2,1,0:T(8,128)(2,1)}, u32[]{:S(2)}, u32[]{:S(2)}) %all-to-all-start.1) | async-done | bytes 8388640 | tf_op jit(solution)/shard_map/all_to_all | solution.py:176
  286.5 0.0 collective-permute-done.2
  286.5 0.0 collective-permute-done.1
  286.5 0.0 collective-permute-done
  286.5 0.0 copy-done.5
  286.5 3.4 %add_convert_fusion = bf16[32,16,1024]{2,1,0:T(8,128)(2,1)} fusion(bf16[32,16,1024]{2,1,0:T(8,128)(2,1)S(1)} %collective-permute-done.2, bf16[32,16,1024]{2,1,0:T(8,128)(2,1)} %collective-permute-done.1, f32[32,16,1024]{2,1,0:T(8,128)S(1)} %copy-done.5, bf16[32,16,1024]{2,1,0:T(8,128)(2,1)} %collective-permute-done), kind=kLoop, calls=%fused_computation.1 | loop fusion | flops 3670016 | bytes 6291456 | tf_op jit(solution)/shard_map/convert_element_type | solution.py:203
  289.9 18.9 %all-to-all-start.2 = ((bf16[32,16,1024]{2,1,0:T(8,128)(2,1)}), bf16[32,16,1024]{2,1,0:T(8,128)(2,1)S(1)}, u32[]{:S(2)}, u32[]{:S(2)}) async-start(bf16[32,16,1024]{2,1,0:T(8,128)(2,1)} %add_convert_fusion), calls=%async_computation.2 | async-start | bytes 2097152 | tf_op jit(solution)/shard_map/all_to_all | solution.py:176
  308.8 0.7 multiply_bitcast_fusion
  309.5 0.1 broadcast_bitcast_fusion
  309.5 0.0 copy-start.1
  309.5 2.2 copy-done.1
  311.7 0.0 copy-start.3
  311.7 2.2 copy-done.3
  313.9 10.2 %shard_map.95 = (bf16[1,32,64,1024]{3,2,1,0:T(8,128)(2,1)}, bf16[1,32,64,1024]{3,2,1,0:T(8,128)(2,1)}) custom-call(bf16[32,2,2,32,1024]{4,3,2,1,0:T(8,128)(2,1)} %all-to-all-done.1.in_ref, bf16[1,32,64,1024]{3,2,1,0:T(8,128)(2,1)S(1)} %copy-done.1, bf16[1,32,64,1024]{3,2,1,0:T(8,128)(2,1)S(1)} %copy-done.3), custom_call_target="tpu_custom_call" | custom-call | tf_op jit(solution)/shard_map/pallas_call | solution.py:79
  324.1 0.1 all-to-all-done.2
  324.2 0.2 convert_reduce_fusion
  324.4 0.6 slice_multiply_fusion
Async XLA Ops:
  0.6 2.2 copy-start
  2.8 2.2 copy-start.2
  5.0 2.2 copy-start.4
  14.3 130.1 %all-to-all-start = ((bf16[32,2,2,32,1024]{4,3,2,1,0:T(8,128)(2,1)}), bf16[32,2,2,32,1024]{4,3,2,1,0:T(8,128)(2,1)}, u32[]{:S(2)}, u32[]{:S(2)}) async-start(bf16[32,2,2,32,1024]{4,3,2,1,0:T(8,128)(2,1)} %shard_map.93), calls=%async_computation | async-start | bytes 16777216 | tf_op jit(solution)/shard_map/all_to_all | solution.py:176
  170.4 116.1 %copy-start.5 = (f32[32,16,1024]{2,1,0:T(8,128)S(1)}, f32[32,16,1024]{2,1,0:T(8,128)}, u32[]{:S(2)}) copy-start(f32[32,16,1024]{2,1,0:T(8,128)} %get-tuple-element.18) | copy-start | bytes 6291460
  170.4 116.1 %all-to-all-start.1 = ((bf16[32,2,2,32,1024]{4,3,2,1,0:T(8,128)(2,1)}), bf16[32,2,2,32,1024]{4,3,2,1,0:T(8,128)(2,1)}, u32[]{:S(2)}, u32[]{:S(2)}) async-start(bf16[32,2,2,32,1024]{4,3,2,1,0:T(8,128)(2,1)} %get-tuple-element.14), calls=%async_computation.1 | async-start | bytes 16777216 | tf_op jit(solution)/shard_map/all_to_all | solution.py:176
  181.4 105.1 %collective-permute-start.2 = (bf16[32,16,1024]{2,1,0:T(8,128)(2,1)}, bf16[32,16,1024]{2,1,0:T(8,128)(2,1)S(1)}, u32[]{:S(2)}, u32[]{:S(2)}) collective-permute-start(bf16[32,16,1024]{2,1,0:T(8,128)(2,1)} %get-tuple-element.21), channel_id=1, source_target_pairs={{0,7},{1,6},{2,5},{3,4},{4,3},{5,2},{6,1},{7,0},{8,15},{9,14},{10,... | collective-permute-start | bytes 3145736 | tf_op jit(solution)/shard_map/ppermute | solution.py:198
  182.2 104.3 %collective-permute-start.1 = (bf16[32,16,1024]{2,1,0:T(8,128)(2,1)}, bf16[32,16,1024]{2,1,0:T(8,128)(2,1)}, u32[]{:S(2)}, u32[]{:S(2)}) collective-permute-start(bf16[32,16,1024]{2,1,0:T(8,128)(2,1)} %get-tuple-element.20), channel_id=1, source_target_pairs={{0,6},{1,7},{2,4},{3,5},{4,2},{5,3},{6,0},{7,1},{8,14},{9,15},{10,... | collective-permute-start | bytes 3145736 | tf_op jit(solution)/shard_map/ppermute | solution.py:198
  184.6 101.9 %collective-permute-start = (bf16[32,16,1024]{2,1,0:T(8,128)(2,1)}, bf16[32,16,1024]{2,1,0:T(8,128)(2,1)}, u32[]{:S(2)}, u32[]{:S(2)}) collective-permute-start(bf16[32,16,1024]{2,1,0:T(8,128)(2,1)} %get-tuple-element.19), channel_id=1, source_target_pairs={{0,1},{1,0},{2,3},{3,2},{4,5},{5,4},{6,7},{7,6},{8,9},{9,8},{10,11... | collective-permute-start | bytes 3145736 | tf_op jit(solution)/shard_map/ppermute | solution.py:198
  289.9 34.4 %all-to-all-start.2 = ((bf16[32,16,1024]{2,1,0:T(8,128)(2,1)}), bf16[32,16,1024]{2,1,0:T(8,128)(2,1)S(1)}, u32[]{:S(2)}, u32[]{:S(2)}) async-start(bf16[32,16,1024]{2,1,0:T(8,128)(2,1)} %add_convert_fusion), calls=%async_computation.2 | async-start | bytes 2097152 | tf_op jit(solution)/shard_map/all_to_all | solution.py:176
  309.5 2.2 copy-start.1
  311.7 2.2 copy-start.3

commit v2 on v1

v2 whole, which is shorter than its diff:
```python
import math

import jax
import jax.numpy as jnp
from jax import lax
from jax.experimental import pallas as pl
from jax.experimental.pallas import tpu as pltpu
from jax.sharding import PartitionSpec as P

BF = jnp.bfloat16
F32 = jnp.float32
MIB = 1024 * 1024
SUB = 16
SIDE = 256


def params(mib):
    return pltpu.CompilerParams(vmem_limit_bytes=mib * MIB)


def shape(dims, dtype):
    return jax.ShapeDtypeStruct(dims, dtype)


def in_hbm(x):
    return pltpu.with_memory_space_constraint(x, pltpu.HBM)


def dot(a, b, on_a, on_b):
    return lax.dot_general(a, b, (((on_a,), (on_b,)), ((), ())), preferred_element_type=F32)


def turn(values):
    size = SUB * SUB
    row = lax.broadcasted_iota(jnp.int32, (size, size), 0)
    col = lax.broadcasted_iota(jnp.int32, (size, size), 1)
    other = row % SUB * SUB + row // SUB
    matrix = jnp.where(col == other, 1.0, 0.0).astype(BF)
    return dot(matrix, values, 1, 0)


def spread_kernel(place_ref, x_ref, cot_ref, gate_ref, out_ref, place_out_ref):
    for k in range(place_ref.shape[0]):
        place_out_ref[k] = place_ref[k]
    size, width = SUB * SUB, x_ref.shape[3]
    dims = (SUB // 2, 2, SUB, width)
    out_ref[:, :, 0] = turn(x_ref[0].reshape(size, width)).astype(BF).reshape(dims)
    sig = jax.nn.sigmoid(gate_ref[0].astype(F32))
    grad = (cot_ref[0].astype(F32) * sig).astype(BF)
    out_ref[:, :, 1] = turn(grad.reshape(size, width)).astype(BF).reshape(dims)


def gather_kernel(in_ref, cot_ref, gate_ref, back_ref, grad_ref):
    size, width = SUB * SUB, cot_ref.shape[3]
    dims = (SUB, SUB, width)
    back_ref[0] = turn(in_ref[:, :, 1].reshape(size, width)).astype(BF).reshape(dims)
    mixed = turn(in_ref[:, :, 0].reshape(size, width)).reshape(dims)
    sig = jax.nn.sigmoid(gate_ref[0].astype(F32))
    cot = cot_ref[0].astype(F32)
    grad_ref[0] = (cot * mixed * sig * (1.0 - sig)).astype(BF)


def retile_specs(dims):
    _, rows, channels, width = dims
    natural = pl.BlockSpec((1, SUB, SUB, width), lambda i, c: (0, i, c, 0))
    apart = pl.BlockSpec((SUB // 2, 2, 2, SUB, width), lambda i, c: (c, 0, 0, i, 0))
    return (rows // SUB, channels // SUB), natural, apart


def spread(place, x, cot, gate):
    _, rows, channels, width = x.shape
    grid, natural, apart = retile_specs(x.shape)
    smem = pl.BlockSpec(memory_space=pltpu.SMEM)
    return pl.pallas_call(
        spread_kernel,
        grid=grid,
        in_specs=[smem] + [natural] * 3,
        out_specs=(apart, smem),
        out_shape=(
            pltpu.HBM((channels // 2, 2, 2, rows, width), BF),
            shape(place.shape, place.dtype),
        ),
        compiler_params=params(40),
    )(place, in_hbm(x), in_hbm(cot), in_hbm(gate))


def gather(parts, cot, gate):
    grid, natural, apart = retile_specs(cot.shape)
    return pl.pallas_call(
        gather_kernel,
        grid=grid,
        in_specs=[apart, natural, natural],
        out_specs=(natural, natural),
        out_shape=(pltpu.HBM(cot.shape, BF), pltpu.HBM(cot.shape, BF)),
        compiler_params=params(40),
    )(in_hbm(parts), in_hbm(cot), in_hbm(gate))


def mask_factor(tiles_ref, in_ref, out_ref):
    count = tiles_ref.shape[0]
    side = in_ref.shape[0] // count
    for a in range(count):
        rows = slice(a * side, (a + 1) * side)
        for b in range(count):
            cols = slice(b * side, (b + 1) * side)
            if b > a:
                out_ref[rows, cols] = jnp.zeros((side, side), BF)
            else:
                value = tiles_ref[a, b].astype(F32)
                out_ref[rows, cols] = (in_ref[rows, cols].astype(F32) * value).astype(BF)


def by_device(part, rows):
    return part.reshape(part.shape[0] // rows, rows, part.shape[1])


def mix_kernel(
    place_ref, tiles_ref, left_ref, right_ref, in_ref,
    out_ref, grad_ref, right_out_ref, keep_ref, give_ref,
    left, left_t, right, first, sum_l, sum_r,
):
    step = pl.program_id(0)

    @pl.when(step == 0)
    def _():
        mask_factor(tiles_ref, left_ref, left)
        mask_factor(tiles_ref, right_ref, right)
        left_t[...] = left[...].T
        right_out_ref[...] = right[...]
        sum_l[...] = jnp.zeros_like(sum_l)
        sum_r[...] = jnp.zeros_like(sum_r)

    width = left.shape[0]
    rows = in_ref.shape[3]
    blocks = [(at, at + SIDE) for at in range(0, width, SIDE)]
    x = in_ref[:, 0, 0].reshape(width, width)
    g = in_ref[:, 0, 1].reshape(width, width)
    for at, end in blocks:
        first[:, at:end] = dot(x[:, :end], right[at:end, :end], 1, 1).astype(BF)
    for at, end in blocks:
        part = dot(left[at:end, :end], first[:end], 1, 0).astype(BF)
        out_ref[at // rows : end // rows, 0, 0] = by_device(part, rows)
    for at, end in blocks:
        part = dot(left_t[at:end, at:], g[at:], 1, 0).astype(BF)
        grad_ref[at // rows : end // rows, 0] = by_device(part, rows)
    grad_first = grad_ref[...].reshape(width, width)

    def add(total, at, end, part):
        _, inner, own, _ = total.shape
        count = SIDE // (inner * own)
        begin = at // (inner * own)
        total[begin : begin + count, :, :, :end] += part.reshape(count, inner, own, end)

    for at, end in blocks:
        add(sum_l, at, end, dot(g[at:end], first[:end], 1, 1))
        add(sum_r, at, end, dot(grad_first[:, at:end], x[:, :end], 0, 0))

    @pl.when(step == 1)
    def _():
        core = place_ref[0] % 2
        for ref, part in ((keep_ref, core), (give_ref, 1 - core)):
            both = (sum_l[:, part], sum_r[:, part])
            ref[...] = jnp.concatenate(both, axis=1).astype(ref.dtype)


def mix(place, tiles, left, right, parts, own):
    devices, _, _, rows, width = parts.shape
    groups = width // (2 * own)
    channel = pl.BlockSpec((devices, 1, 2, rows, width), lambda c: (0, c, 0, 0, 0))
    mixed = pl.BlockSpec((devices, 1, 1, rows, width), lambda c: (0, c, 0, 0, 0))
    grad = pl.BlockSpec((devices, 1, rows, width), lambda c: (0, c, 0, 0))
    factor = pl.BlockSpec((width, width), lambda c: (0, 0))
    half = pl.BlockSpec((groups, 2 * own, width), lambda c: (0, 0, 0))
    smem = pl.BlockSpec(memory_space=pltpu.SMEM)
    square = pltpu.VMEM((width, width), BF)
    total = pltpu.VMEM((groups, 2, own, width), F32)
    dims = (groups, 2 * own, width)
    return pl.pallas_call(
        mix_kernel,
        grid=(2,),
        in_specs=[smem, smem, factor, factor, channel],
        out_specs=(mixed, grad, factor, half, half),
        out_shape=(
            pltpu.HBM(parts.shape, BF),
            pltpu.HBM((devices, 2, rows, width), BF),
            pltpu.HBM((width, width), BF),
            pltpu.HBM(dims, F32),
            pltpu.HBM(dims, BF),
        ),
        scratch_shapes=[square, square, square, square, total, total],
        compiler_params=params(62),
    )(place, tiles, in_hbm(left), in_hbm(right), in_hbm(parts))


def back_kernel(right_ref, grad_ref, parts_ref, out_ref):
    width = right_ref.shape[0]
    rows = grad_ref.shape[2]
    grad_first = grad_ref[...].reshape(width, width)
    for at in range(0, width, SIDE):
        end = at + SIDE
        part = dot(grad_first[:, at:], right_ref[at:, at:end], 1, 0).astype(BF)
        out_ref[:, 0, 0, :, at:end] = by_device(part, rows)


def back(right, grad_first, parts):
    devices, _, _, rows, width = parts.shape
    return pl.pallas_call(
        back_kernel,
        grid=(2,),
        in_specs=[
            pl.BlockSpec((width, width), lambda c: (0, 0)),
            pl.BlockSpec((devices, 1, rows, width), lambda c: (0, c, 0, 0)),
            pl.BlockSpec(memory_space=pl.ANY),
        ],
        out_specs=pl.BlockSpec((devices, 1, 1, rows, width), lambda c: (0, c, 1, 0, 0)),
        out_shape=pltpu.HBM(parts.shape, BF),
        input_output_aliases={2: 0},
        compiler_params=params(40),
    )(in_hbm(right), in_hbm(grad_first), in_hbm(parts))


def add_kernel(keep_ref, got_ref, parts_ref, sum_ref, parts_out_ref):
    sum_ref[...] = (keep_ref[...] + got_ref[...].astype(F32)).astype(BF)


def add(keep, got, parts):
    groups, rows, width = keep.shape
    step = groups // 4
    block = pl.BlockSpec((step, rows, width), lambda g: (g, 0, 0))
    whole = pl.BlockSpec(memory_space=pl.ANY)
    return pl.pallas_call(
        add_kernel,
        grid=(4,),
        in_specs=[block, block, whole],
        out_specs=(block, whole),
        out_shape=(pltpu.HBM(keep.shape, BF), pltpu.HBM(parts.shape, BF)),
        input_output_aliases={2: 1},
        compiler_params=params(16),
    )(in_hbm(keep), in_hbm(got), in_hbm(parts))


def tie_kernel(total_ref, parts_ref, out_ref):
    pass


def tie(total, parts):
    whole = pl.BlockSpec(memory_space=pl.ANY)
    return pl.pallas_call(
        tie_kernel,
        in_specs=[whole, whole],
        out_specs=whole,
        out_shape=pltpu.HBM(total.shape, BF),
        input_output_aliases={0: 0},
    )(in_hbm(total), in_hbm(parts))


def finish_kernel(count, scale, place_ref, tiles_ref, in_ref, left_ref, right_ref):
    own, width = left_ref.shape
    side = width // tiles_ref.shape[0]
    row = (place_ref[1] * count + place_ref[0]) * own // side
    sums = jnp.sum(in_ref[...].astype(F32), 0)
    for tile in range(tiles_ref.shape[0]):
        lanes = slice(tile * side, (tile + 1) * side)
        factor = tiles_ref[row, tile].astype(F32) * scale
        left_ref[:, lanes] = sums[:own, lanes] * factor
        right_ref[:, lanes] = sums[own:, lanes] * factor


def finish(place, tiles, total, count, scale):
    _, both, width = total.shape
    smem = pl.BlockSpec(memory_space=pltpu.SMEM)
    vmem = pl.BlockSpec(memory_space=pltpu.VMEM)
    out = shape((both // 2, width), F32)
    return pl.pallas_call(
        lambda *refs: finish_kernel(count, scale, *refs),
        in_specs=[smem, smem, vmem],
        out_specs=(vmem, vmem),
        out_shape=(out, out),
        compiler_params=params(16),
    )(place, tiles, total)


def swap(x):
    return lax.all_to_all(x, "seq", split_axis=0, concat_axis=0, tiled=True)


def shards(inputs, gate_in, cotangent, right_factor, left_factor, mask_tiles):
    width = right_factor.shape[0]
    channels = inputs.shape[2]
    seq_count = lax.axis_size("seq")
    data_count = lax.axis_size("dp")
    own = width // (seq_count * data_count)
    place = jnp.stack((lax.axis_index("dp"), lax.axis_index("seq"))).astype(jnp.int32)

    parts, place = spread(place, inputs, cotangent, gate_in)
    parts = swap(parts)
    mixed, grad_first, right, keep, give = mix(
        place, mask_tiles, left_factor, right_factor, parts, own
    )
    got = lax.ppermute(give, "dp", [(d, d ^ 1) for d in range(data_count)])
    parts = back(right, grad_first, mixed)
    total, parts = add(keep, got, parts)
    parts = swap(parts)
    total = tie(total, parts)
    same_core = [
        [s * data_count + d for s in range(seq_count) for d in range(core, data_count, 2)]
        for core in range(2)
    ]
    total = lax.all_to_all(
        total,
        ("seq", "dp"),
        split_axis=0,
        concat_axis=0,
        tiled=True,
        axis_index_groups=same_core,
    )
    grad_input, grad_gate = gather(parts, cotangent, gate_in)
    scale = 1.0 / math.sqrt(data_count * channels * width)
    grad_left, grad_right = finish(place, mask_tiles, total, data_count, scale)
    return grad_input, grad_gate, grad_right, grad_left


def solution(mesh):
    placed = (
        P("dp", "seq", None, None),
        P("dp", "seq", None, None),
        P("dp", "seq", None, None),
        P(),
        P(),
        P(),
    )
    return jax.shard_map(
        shards,
        mesh=mesh,
        in_specs=placed,
        out_specs=(
            P("dp", "seq", None, None),
            P("dp", "seq", None, None),
            P(("seq", "dp"), None),
            P(("seq", "dp"), None),
        ),
        check_vma=False,
    )
```

time: 326 us -> 302 us (0.926)
  blocking collectives: 0 us -> 209 us
  waiting for transfers between devices: 223 us -> 17.6 us
  starting transfers between devices: 42.5 us -> 11.4 us
  Pallas kernels: 43.3 us -> 61.6 us
  local copies, waits for them, and re-layouts: 11 us -> 1.34 us
  other arithmetic: 4.84 us -> 0.08 us
    all_to_all x0 -> x2, blocking collectives: none -> 209 us  [swap(): return lax.all_to_all(x, 'seq', split_axis=0, concat_axis=0, tiled=True)]
    all_to_all x3 -> x1, waiting for transfers between devices: 223 us -> 17.6 us  [shards(): lax.all_to_all(total, ('seq', 'dp'), split_axis=0, concat_axis=0, tiled=T...]
    all_to_all x3 -> x1, starting transfers between devices: 39.2 us -> 11.3 us  [shards(): lax.all_to_all(total, ('seq', 'dp'), split_axis=0, concat_axis=0, tiled=T...]
    pallas_call x1 -> x5, Pallas kernels: 7.07 us -> 24.1 us  [the longest x1 11.3 us: spread(): pl.pallas_call(spread_kernel, grid=grid, in_specs=[smem] + [natural] * 3,...]
    unnamed x12 -> x8, local copies, waits for them, and re-layouts: 10.9 us -> 1.34 us
    convert_element_type x1 -> x0, other arithmetic: 3.35 us -> none  [shards(): total = swap(total.astype(BF))]
  transfers between devices with their start and end apart: 6 -> 2, of which waited for: 3 -> 1; matrix products, arithmetic and copies ran while one was open for 0% -> 0% of each run, Pallas kernels for 3% -> 6%
where the time goes in v2:
time: 302 us; the launch traced here: 301 us
  blocking collectives  209 us (69%)
  Pallas kernels  61.6 us (20%)
  waiting for transfers between devices  17.6 us (6%)
  starting transfers between devices  11.4 us (4%)
    all_to_all x2, blocking collectives, swap(): return lax.all_to_all(x, 'seq', split_axis=0, concat_axis=0, tiled=True)  209 us
    pallas_call x1, Pallas kernels, mix(): pl.pallas_call(mix_kernel, grid=(2,), in_specs=[smem, smem, factor, facto...  25.1 us
    all_to_all x1, waiting for transfers between devices, shards(): lax.all_to_all(total, ('seq', 'dp'), split_axis=0, concat_axis=0, tiled=T...  17.6 us
    pallas_call x1, Pallas kernels, gather(): pl.pallas_call(gather_kernel, grid=grid, in_specs=[apart, natural, natura...  12.4 us
    pallas_call x1, Pallas kernels, spread(): pl.pallas_call(spread_kernel, grid=grid, in_specs=[smem] + [natural] * 3,...  11.3 us
    all_to_all x1, starting transfers between devices, shards(): lax.all_to_all(total, ('seq', 'dp'), split_axis=0, concat_axis=0, tiled=T...  11.3 us
    pallas_call x1, Pallas kernels, back(): pl.pallas_call(back_kernel, grid=(2,), in_specs=[pl.BlockSpec((width, wid...  6.6 us
  transfers between devices with their start and end apart: 2, of which 1 were waited for; matrix products, arithmetic and copies ran while one was open for 0% of the time, Pallas kernels for 6%

profile of v2, /device:TPU:0, one launch (start us, length us, event | category | flops | bytes accessed | tf_op | source)
XLA Modules:
  0.0 301.4 jit_solution(14281193352790782604)
XLA Ops:
  0.6 0.1 pad_add_fusion.place_ref
  0.7 11.3 %shard_map.93 = (bf16[32,2,2,32,1024]{4,3,2,1,0:T(8,128)(2,1)}, s32[2]{0:T(128)S(1)}) custom-call(s32[2]{0:T(128)S(1)} %pad_add_fusion.place_ref, bf16[1,32,64,1024]{3,2,1,0:T(8,128)(2,1)} %x_ref.1, bf16[1,32,64,1024]{3,2,1,0:T(8,128)(2,1)} %cot_ref.3, bf16[1,32,64,1024]{3,2,1,0:T(8,128)(2,1)} %gate_ref.3), custom_call_target="tpu_custom_call" | custom-call | tf_op jit(solution)/shard_map/pallas_call | solution.py:74
  12.0 0.0 copy-start.1
  12.0 105.9 %all_to_all.15.in_ref = bf16[32,2,2,32,1024]{4,3,2,1,0:T(8,128)(2,1)} all-to-all(bf16[32,2,2,32,1024]{4,3,2,1,0:T(8,128)(2,1)} %get-tuple-element.18), channel_id=1, replica_groups=mesh['seq'=32,'dp'=4] {'seq'}, dimensions={0} | all-to-all | bytes 16777216 | tf_op jit(solution)/shard_map/all_to_all | solution.py:284
  117.9 0.0 copy-done.1
  117.9 25.1 %shard_map.94 = (bf16[32,2,2,32,1024]{4,3,2,1,0:T(8,128)(2,1)}, bf16[32,2,32,1024]{3,2,1,0:T(8,128)(2,1)}, bf16[1024,1024]{1,0:T(8,128)(2,1)}, f32[64,16,1024]{2,1,0:T(8,128)}, bf16[64,16,1024]{2,1,0:T(8,128)(2,1)}) custom-call(s32[2]{0:T(128)} %copy-done.1, s32[8,8]{1,0:T(8,128)} %refs_1_.1, bf16[1024,1024]{1,0:T(8,128)(2,1)} %left_ref.1, ...), custom_call_target="tpu_custom_call" | custom-call | tf_op jit(solution)/shard_map/pallas_call | solution.py:178
  143.0 0.1 collective-permute-start
  143.1 6.6 %shard_map.95.parts_ref = bf16[32,2,2,32,1024]{4,3,2,1,0:T(8,128)(2,1)} custom-call(bf16[1024,1024]{1,0:T(8,128)(2,1)} %get-tuple-element.21.right_ref, bf16[32,2,32,1024]{3,2,1,0:T(8,128)(2,1)} %get-tuple-element.22.grad_ref, bf16[32,2,2,32,1024]{4,3,2,1,0:T(8,128)(2,1)} %get-tuple-element.23.parts_ref), custom_call_target="tpu_custom_call", output_to_operand_aliasing={{}: (2, {})} | custom-call | tf_op jit(solution)/shard_map/pallas_call | solution.py:207
  149.7 0.0 collective-permute-done.got_ref
  149.7 0.0 copy-start.3
  149.7 1.3 copy-done.3
  151.0 4.6 %shard_map.96 = (bf16[64,16,1024]{2,1,0:T(8,128)(2,1)}, bf16[32,2,2,32,1024]{4,3,2,1,0:T(8,128)(2,1)}) custom-call(f32[64,16,1024]{2,1,0:T(8,128)} %get-tuple-element.19.keep_ref, bf16[64,16,1024]{2,1,0:T(8,128)(2,1)} %copy-done.3, bf16[32,2,2,32,1024]{4,3,2,1,0:T(8,128)(2,1)} %shard_map.95.parts_ref), custom_call_target="tpu_custom_call", output_to_operand_aliasing={{1}: (2, {})} | custom-call | tf_op jit(solution)/shard_map/pallas_call | solution.py:231
  155.6 102.9 %all_to_all.16.in_ref.parts_ref = bf16[32,2,2,32,1024]{4,3,2,1,0:T(8,128)(2,1)} all-to-all(bf16[32,2,2,32,1024]{4,3,2,1,0:T(8,128)(2,1)} %get-tuple-element.24), channel_id=1, replica_groups=mesh['seq'=32,'dp'=4] {'seq'}, dimensions={0} | all-to-all | bytes 16777216 | tf_op jit(solution)/shard_map/all_to_all | solution.py:284
  258.5 11.3 %all-to-all-start.2 = ((bf16[64,16,1024]{2,1,0:T(8,128)(2,1)}), bf16[64,16,1024]{2,1,0:T(8,128)(2,1)S(1)}, u32[]{:S(2)}, u32[]{:S(2)}) async-start(bf16[64,16,1024]{2,1,0:T(8,128)(2,1)} %shard_map.98), calls=%async_computation.2 | async-start | bytes 4194304 | tf_op jit(solution)/shard_map/all_to_all | solution.py:309
  269.8 0.0 copy-start
  269.8 0.0 copy-start.2
  269.8 12.4 %shard_map.97 = (bf16[1,32,64,1024]{3,2,1,0:T(8,128)(2,1)}, bf16[1,32,64,1024]{3,2,1,0:T(8,128)(2,1)}) custom-call(bf16[32,2,2,32,1024]{4,3,2,1,0:T(8,128)(2,1)} %all_to_all.16.in_ref.parts_ref, bf16[1,32,64,1024]{3,2,1,0:T(8,128)(2,1)} %cot_ref.3, bf16[1,32,64,1024]{3,2,1,0:T(8,128)(2,1)} %gate_ref.3), custom_call_target="tpu_custom_call" | custom-call | tf_op jit(solution)/shard_map/pallas_call | solution.py:89
  282.2 17.6 %all-to-all-done.2.refs_2_ = bf16[64,16,1024]{2,1,0:T(8,128)(2,1)S(1)} async-done(((bf16[64,16,1024]{2,1,0:T(8,128)(2,1)}), bf16[64,16,1024]{2,1,0:T(8,128)(2,1)S(1)}, u32[]{:S(2)}, u32[]{:S(2)}) %all-to-all-start.2) | async-done | bytes 2097184 | tf_op jit(solution)/shard_map/all_to_all | solution.py:309
  299.8 0.0 copy-done
  299.8 0.0 copy-done.2
  299.8 1.6 shard_map.99
  (1 shorter events, 0.0 us)
Async XLA Ops:
  12.0 105.9 %copy-start.1 = (s32[2]{0:T(128)}, s32[2]{0:T(128)S(1)}, u32[]{:S(2)}) copy-start(s32[2]{0:T(128)S(1)} %get-tuple-element.17.place_ref.refs_0_) | copy-start | bytes 28
  143.0 6.7 %collective-permute-start = (bf16[64,16,1024]{2,1,0:T(8,128)(2,1)}, bf16[64,16,1024]{2,1,0:T(8,128)(2,1)S(1)}, u32[]{:S(2)}, u32[]{:S(2)}) collective-permute-start(bf16[64,16,1024]{2,1,0:T(8,128)(2,1)} %get-tuple-element.20), channel_id=1, source_target_pairs={{0,1},{1,0},{2,3},{3,2},{4,5},{5,4},{6,7},{7,6},{8,9},{9,8},{10,11... | collective-permute-start | bytes 6291464 | tf_op jit(solution)/shard_map/ppermute | solution.py:300
  149.7 1.3 copy-start.3
  258.5 41.3 %all-to-all-start.2 = ((bf16[64,16,1024]{2,1,0:T(8,128)(2,1)}), bf16[64,16,1024]{2,1,0:T(8,128)(2,1)S(1)}, u32[]{:S(2)}, u32[]{:S(2)}) async-start(bf16[64,16,1024]{2,1,0:T(8,128)(2,1)} %shard_map.98), calls=%async_computation.2 | async-start | bytes 4194304 | tf_op jit(solution)/shard_map/all_to_all | solution.py:309
  269.8 30.1 %copy-start = (s32[8,8]{1,0:T(8,128)S(1)}, s32[8,8]{1,0:T(8,128)}, u32[]{:S(2)}) copy-start(s32[8,8]{1,0:T(8,128)} %refs_1_.1) | copy-start | bytes 772
  269.8 30.1 %copy-start.2 = (s32[2]{0:T(128)S(1)}, s32[2]{0:T(128)}, u32[]{:S(2)}) copy-start(s32[2]{0:T(128)} %copy-done.1) | copy-start | bytes 28

commit v3 on v2

v3 whole, which is shorter than its diff:
```python
import math

import jax
import jax.numpy as jnp
from jax import lax
from jax.experimental import pallas as pl
from jax.experimental.pallas import tpu as pltpu
from jax.sharding import PartitionSpec as P

BF = jnp.bfloat16
F32 = jnp.float32
MIB = 1024 * 1024
LANES = 128
SUB = 16
SIDE = 256


def params(mib):
    return pltpu.CompilerParams(vmem_limit_bytes=mib * MIB)


def shape(dims, dtype):
    return jax.ShapeDtypeStruct(dims, dtype)


def in_hbm(x):
    return pltpu.with_memory_space_constraint(x, pltpu.HBM)


def dot(a, b, on_a, on_b):
    return lax.dot_general(a, b, (((on_a,), (on_b,)), ((), ())), preferred_element_type=F32)


def turn(values):
    size = SUB * SUB
    row = lax.broadcasted_iota(jnp.int32, (size, size), 0)
    col = lax.broadcasted_iota(jnp.int32, (size, size), 1)
    other = row % SUB * SUB + row // SUB
    matrix = jnp.where(col == other, 1.0, 0.0).astype(BF)
    return dot(matrix, values, 1, 0)


def spread_kernel(place_ref, x_ref, cot_ref, gate_ref, out_ref, place_out_ref):
    for k in range(place_ref.shape[0]):
        place_out_ref[k] = place_ref[k]
    size, width = SUB * SUB, x_ref.shape[3]
    dims = (SUB // 2, 2, SUB, width)
    for at in range(0, x_ref.shape[1], SUB):
        rows = slice(at, at + SUB)
        part = turn(x_ref[0, rows].reshape(size, width))
        out_ref[:, :, 0, rows] = part.astype(BF).reshape(dims)
        tanh = jnp.tanh(gate_ref[0, rows].astype(F32) * 0.5)
        grad = (cot_ref[0, rows].astype(F32) * (0.5 + 0.5 * tanh)).astype(BF)
        part = turn(grad.reshape(size, width))
        out_ref[:, :, 1, rows] = part.astype(BF).reshape(dims)


def spread(place, x, cot, gate):
    _, rows, channels, width = x.shape
    natural = pl.BlockSpec((1, rows, SUB, width), lambda c: (0, 0, c, 0))
    smem = pl.BlockSpec(memory_space=pltpu.SMEM)
    return pl.pallas_call(
        spread_kernel,
        grid=(channels // SUB,),
        in_specs=[smem] + [natural] * 3,
        out_specs=(
            pl.BlockSpec((SUB // 2, 2, 2, rows, width), lambda c: (c, 0, 0, 0, 0)),
            smem,
        ),
        out_shape=(
            pltpu.HBM((channels // 2, 2, 2, rows, width), BF),
            shape(place.shape, place.dtype),
        ),
        compiler_params=params(48),
    )(place, in_hbm(x), in_hbm(cot), in_hbm(gate))


def gather_kernel(in_ref, cot_ref, gate_ref, after_ref, back_ref, grad_ref):
    size, width = SUB * SUB, cot_ref.shape[3]
    dims = (SUB, SUB, width)
    tiles = width // LANES
    halves = cot_ref.shape[1] // SUB

    def rows_of(array, half):
        columns = []
        for tile in range(tiles):
            at = [((c * 2 + array) * tiles + tile) * halves + half for c in range(2)]
            both = jnp.stack((in_ref[:, at[0]], in_ref[:, at[1]]), 1)
            columns.append(both.reshape(size, LANES))
        return turn(jnp.concatenate(columns, 1))

    for half in range(halves):
        rows = slice(half * SUB, (half + 1) * SUB)
        back_ref[0, rows] = rows_of(1, half).astype(BF).reshape(dims)
        mixed = rows_of(0, half).reshape(dims)
        tanh = jnp.tanh(gate_ref[0, rows].astype(F32) * 0.5)
        slope = 0.25 * (1.0 - tanh) * (1.0 + tanh)
        grad_ref[0, rows] = (cot_ref[0, rows].astype(F32) * mixed * slope).astype(BF)


def gather(parts, cot, gate, after):
    _, rows, channels, width = cot.shape
    natural = pl.BlockSpec((1, rows, SUB, width), lambda c: (0, 0, c, 0))
    blocks = 4 * rows * width // (SUB * LANES)
    return pl.pallas_call(
        gather_kernel,
        grid=(channels // SUB,),
        in_specs=[
            pl.BlockSpec((SUB // 2, blocks, SUB, LANES), lambda c: (c, 0, 0, 0)),
            natural,
            natural,
            pl.BlockSpec(memory_space=pl.ANY),
        ],
        out_specs=(natural, natural),
        out_shape=(pltpu.HBM(cot.shape, BF), pltpu.HBM(cot.shape, BF)),
        compiler_params=params(48),
    )(in_hbm(parts), in_hbm(cot), in_hbm(gate), after)


def mask_factor(tiles_ref, ref):
    count = tiles_ref.shape[0]
    side = ref.shape[0] // count
    for a in range(count):
        rows = slice(a * side, (a + 1) * side)
        for b in range(count):
            cols = slice(b * side, (b + 1) * side)
            if b > a:
                ref[rows, cols] = jnp.zeros((side, side), BF)
            else:
                value = tiles_ref[a, b].astype(F32)
                ref[rows, cols] = (ref[rows, cols].astype(F32) * value).astype(BF)


def put_tiles(ref, lead, part, rows):
    devices, halves = part.shape[0] // rows, rows // SUB
    for tile in range(part.shape[1] // LANES):
        piece = part[:, tile * LANES : (tile + 1) * LANES]
        at = tile * halves
        ref[lead : lead + devices, at : at + halves] = piece.reshape(devices, halves, SUB, LANES)


def mix_kernel(
    place_ref, tiles_ref, left_hbm, right_hbm, in_hbm_ref,
    out_hbm, grad_hbm, right_out_hbm, keep_hbm, give_hbm,
    left, right, xs, gs, first, grad, mixed, total, keep, give, in_sems, out_sems,
):
    width = left.shape[0]
    rows = xs.shape[2]
    devices = width // rows
    blocks = [(at, at + SIDE) for at in range(0, width, SIDE)]

    loads = [
        pltpu.make_async_copy(src, dst, in_sems.at[k])
        for k, (src, dst) in enumerate(
            (
                (right_hbm, right),
                (in_hbm_ref.at[:, 0, 0], xs.at[0]),
                (in_hbm_ref.at[:, 1, 0], xs.at[1]),
                (left_hbm, left),
                (in_hbm_ref.at[:, 0, 1], gs.at[0]),
                (in_hbm_ref.at[:, 1, 1], gs.at[1]),
            )
        )
    ]
    for load in loads:
        load.start()
    stores = []

    def store(src, dst):
        copy = pltpu.make_async_copy(src, dst, out_sems.at[len(stores)])
        copy.start()
        stores.append(copy)

    loads[0].wait()
    mask_factor(tiles_ref, right)
    store(right, right_out_hbm)
    for c in range(2):
        loads[1 + c].wait()
        x = xs[c].reshape(width, width)
        for at, end in blocks:
            first[c, :, at:end] = dot(x[:, :end], right[at:end, :end], 1, 1).astype(BF)
    loads[3].wait()
    mask_factor(tiles_ref, left)
    for c in range(2):
        loads[4 + c].wait()
        g = gs[c].reshape(width, width)
        for at, end in blocks:
            grad[c, at:end] = dot(left[at:, at:end], g[at:], 0, 0).astype(BF)
        store(grad.at[c], grad_hbm.at[c])

    core = place_ref[0] % 2
    side = width // tiles_ref.shape[0]
    per_tile = devices * side // width
    for at, end in blocks:
        sums = [None, None]
        for c in range(2):
            x, g = xs[c].reshape(width, width), gs[c].reshape(width, width)
            left_part = dot(g[at:end], first[c, :end], 1, 1)
            right_part = dot(grad[c, :, at:end], x[:, :end], 0, 0)
            for k, part in enumerate((left_part, right_part)):
                sums[k] = part if sums[k] is None else sums[k] + part
        for k in range(2):
            total[k, :, :, :, :, :end] = sums[k].reshape(total.shape[1:5] + (end,))
        for s in range(at // rows, end // rows):
            lower = s < devices // 2
            mirror = devices - 1 - s
            first_tile = 0 if lower else (mirror // per_tile) + 1
            for k in range(2):
                to = (s if lower else mirror) if k == 0 else (mirror if lower else s)
                for tile in range(s // per_tile + 1):
                    cols = slice(tile * LANES, (tile + 1) * LANES)
                    place = first_tile + tile
                    own = total[k, s - at // rows, :, core, :, cols]
                    keep[to, place] = own.reshape(SUB, LANES)
                    other = total[k, s - at // rows, :, 1 - core, :, cols]
                    give[to, place] = other.reshape(SUB, LANES).astype(BF)
    store(keep, keep_hbm)
    store(give, give_hbm)

    count = mixed.shape[2]
    for c in range(2):
        for at, end in blocks:
            part = dot(left[at:end, :end], first[c, :end], 1, 0).astype(BF)
            put_tiles(mixed.at[c], at // rows, part, rows)
        store(mixed.at[c], out_hbm.at[:, pl.ds(2 * c * count, count)])
    for copy in stores:
        copy.wait()


def mix(place, tiles, left, right, parts, own):
    devices, _, _, rows, width = parts.shape
    halves = rows // SUB
    count = width // LANES * halves
    terms = tiles.shape[0] + 1
    smem = pl.BlockSpec(memory_space=pltpu.SMEM)
    whole = pl.BlockSpec(memory_space=pl.ANY)
    square = pltpu.VMEM((width, width), BF)
    channels = pltpu.VMEM((2, devices, rows, width), BF)
    squares = pltpu.VMEM((2, width, width), BF)
    dims = (devices, terms, SUB, LANES)
    return pl.pallas_call(
        mix_kernel,
        in_specs=[smem, smem, whole, whole, whole],
        out_specs=(whole,) * 5,
        out_shape=(
            pltpu.HBM((devices, 4 * count + terms, SUB, LANES), BF),
            pltpu.HBM((2, width, width), BF),
            pltpu.HBM((width, width), BF),
            pltpu.HBM(dims, F32),
            pltpu.HBM(dims, BF),
        ),
        scratch_shapes=[
            square,
            square,
            channels,
            channels,
            squares,
            squares,
            pltpu.VMEM((2, devices, count, SUB, LANES), BF),
            pltpu.VMEM((2, SIDE // rows, halves, 2, own, width), F32),
            pltpu.VMEM(dims, F32),
            pltpu.VMEM(dims, BF),
            pltpu.SemaphoreType.DMA((6,)),
            pltpu.SemaphoreType.DMA((7,)),
        ],
        compiler_params=params(56),
    )(place, tiles, in_hbm(left), in_hbm(right), in_hbm(parts))


def back_kernel(rows, right_ref, grad_ref, parts_ref, out_ref):
    width = right_ref.shape[0]
    for at in range(0, width, SIDE):
        end = at + SIDE
        part = dot(grad_ref[0, :, at:], right_ref[at:, at:end], 1, 0).astype(BF)
        halves = rows // SUB
        for tile in range(SIDE // LANES):
            piece = part[:, tile * LANES : (tile + 1) * LANES]
            place = (at // LANES + tile) * halves
            out_ref[:, place : place + halves] = piece.reshape(-1, halves, SUB, LANES)


def back(right, grad_first, parts, rows):
    _, width, _ = grad_first.shape
    devices = parts.shape[0]
    count = width // LANES * (rows // SUB)
    return pl.pallas_call(
        lambda *refs: back_kernel(rows, *refs),
        grid=(2,),
        in_specs=[
            pl.BlockSpec((width, width), lambda c: (0, 0)),
            pl.BlockSpec((1, width, width), lambda c: (c, 0, 0)),
            pl.BlockSpec(memory_space=pl.ANY),
        ],
        out_specs=pl.BlockSpec((devices, count, SUB, LANES), lambda c: (0, 2 * c + 1, 0, 0)),
        out_shape=pltpu.HBM(parts.shape, BF),
        input_output_aliases={2: 0},
        compiler_params=params(40),
    )(in_hbm(right), in_hbm(grad_first), in_hbm(parts))


def add_kernel(keep_ref, got_ref, parts_ref, out_ref, total, sem):
    total[...] = (keep_ref[...] + got_ref[...].astype(F32)).astype(BF)
    terms = total.shape[1]
    copy = pltpu.make_async_copy(
        total, out_ref.at[:, pl.ds(out_ref.shape[1] - terms, terms)], sem
    )
    copy.start()
    copy.wait()


def add(keep, got, parts):
    vmem = pl.BlockSpec(memory_space=pltpu.VMEM)
    whole = pl.BlockSpec(memory_space=pl.ANY)
    return pl.pallas_call(
        add_kernel,
        in_specs=[vmem, vmem, whole],
        out_specs=whole,
        out_shape=pltpu.HBM(parts.shape, BF),
        input_output_aliases={2: 0},
        scratch_shapes=[pltpu.VMEM(keep.shape, BF), pltpu.SemaphoreType.DMA],
        compiler_params=params(16),
    )(keep, got, in_hbm(parts))


def fold_kernel(place_ref, parts_ref, mine_ref, other_ref, got, total, sem):
    terms, own = mine_ref.shape[0], mine_ref.shape[1]
    copy = pltpu.make_async_copy(
        parts_ref.at[:, pl.ds(parts_ref.shape[1] - terms, terms)], got, sem
    )
    copy.start()
    copy.wait()
    total[...] = jnp.sum(got[...].astype(F32), 0).reshape(terms, 2, own, LANES)
    high = place_ref[0] // 2
    mine_ref[...] = total[:, high]
    other_ref[...] = total[:, 1 - high]


def fold(place, parts, terms, own):
    vmem = pl.BlockSpec(memory_space=pltpu.VMEM)
    out = shape((terms, own, LANES), F32)
    return pl.pallas_call(
        fold_kernel,
        in_specs=[pl.BlockSpec(memory_space=pltpu.SMEM), pl.BlockSpec(memory_space=pl.ANY)],
        out_specs=(vmem, vmem),
        out_shape=(out, out),
        scratch_shapes=[
            pltpu.VMEM((parts.shape[0], terms, SUB, LANES), BF),
            pltpu.VMEM((terms, 2, own, LANES), F32),
            pltpu.SemaphoreType.DMA,
        ],
        compiler_params=params(16),
    )(place, in_hbm(parts))


def finish_kernel(devices, scale, place_ref, tiles_ref, a_ref, b_ref, c_ref, d_ref, *refs):
    left_ref, right_ref, near, far = refs
    near[...] = a_ref[...] + b_ref[...]
    far[...] = c_ref[...] + d_ref[...]
    count = tiles_ref.shape[0]
    row = place_ref[1] // (devices // count)
    lower = place_ref[1] < devices // 2
    start = jnp.where(lower, 0, count - row)

    def write(left, right):
        for tile in range(count):
            lanes = slice(tile * LANES, (tile + 1) * LANES)
            factor = tiles_ref[row, tile].astype(F32) * scale
            at = jnp.minimum(start + tile, count)
            left_ref[:, lanes] = left[at] * factor
            right_ref[:, lanes] = right[at] * factor

    @pl.when(lower)
    def _():
        write(near, far)

    @pl.when(jnp.logical_not(lower))
    def _():
        write(far, near)


def finish(place, tiles, pieces, devices, scale):
    terms, own, _ = pieces[0].shape
    smem = pl.BlockSpec(memory_space=pltpu.SMEM)
    vmem = pl.BlockSpec(memory_space=pltpu.VMEM)
    out = shape((own, (terms - 1) * LANES), F32)
    slab = pltpu.VMEM((terms, own, LANES), F32)
    return pl.pallas_call(
        lambda *refs: finish_kernel(devices, scale, *refs),
        in_specs=[smem, smem] + [vmem] * 4,
        out_specs=(vmem, vmem),
        out_shape=(out, out),
        scratch_shapes=[slab, slab],
        compiler_params=params(16),
    )(place, tiles, *pieces)


def swap(x):
    return lax.all_to_all(x, "seq", split_axis=0, concat_axis=0, tiled=True)


def shards(inputs, gate_in, cotangent, right_factor, left_factor, mask_tiles):
    width = right_factor.shape[0]
    rows, channels = inputs.shape[1], inputs.shape[2]
    seq_count = lax.axis_size("seq")
    data_count = lax.axis_size("dp")
    own = width // (seq_count * data_count)
    place = jnp.stack((lax.axis_index("dp"), lax.axis_index("seq"))).astype(jnp.int32)

    parts, place = spread(place, inputs, cotangent, gate_in)
    parts = swap(parts)
    mixed, grad_first, right, keep, give = mix(
        place, mask_tiles, left_factor, right_factor, parts, own
    )
    got = lax.ppermute(give, "dp", [(d, d ^ 1) for d in range(data_count)])
    parts = back(right, grad_first, mixed, rows)
    parts = add(keep, got, parts)
    parts = swap(parts)
    mine, other = fold(place, parts, mask_tiles.shape[0] + 1, own)

    def move(x, mirror, flip):
        pairs = [
            (
                s * data_count + d,
                (seq_count - 1 - s if mirror else s) * data_count + (d ^ flip),
            )
            for s in range(seq_count)
            for d in range(data_count)
        ]
        return lax.ppermute(x, ("seq", "dp"), pairs)

    pieces = (mine, move(other, False, 2), move(mine, True, 0), move(other, True, 2))
    grad_input, grad_gate = gather(parts, cotangent, gate_in, mine)
    scale = 1.0 / math.sqrt(data_count * channels * width)
    grad_left, grad_right = finish(place, mask_tiles, pieces, seq_count, scale)
    return grad_input, grad_gate, grad_right, grad_left


def solution(mesh):
    placed = (
        P("dp", "seq", None, None),
        P("dp", "seq", None, None),
        P("dp", "seq", None, None),
        P(),
        P(),
        P(),
    )
    return jax.shard_map(
        shards,
        mesh=mesh,
        in_specs=placed,
        out_specs=(
            P("dp", "seq", None, None),
            P("dp", "seq", None, None),
            P(("seq", "dp"), None),
            P(("seq", "dp"), None),
        ),
        check_vma=False,
    )
```

time: 302 us -> 288 us (0.954)
  waiting for transfers between devices: 17.6 us -> 0.01 us
  blocking collectives: 209 us -> 222 us
  Pallas kernels: 61.6 us -> 53.7 us
    all_to_all x1 -> x0, waiting for transfers between devices: 17.6 us -> none  [shards(): lax.all_to_all(total, ('seq', 'dp'), split_axis=0, concat_axis=0, tiled=T...]
    all_to_all x2, blocking collectives: 209 us -> 222 us  [swap(): return lax.all_to_all(x, 'seq', split_axis=0, concat_axis=0, tiled=True)]
    all_to_all x1 -> x0, starting transfers between devices: 11.3 us -> none  [shards(): lax.all_to_all(total, ('seq', 'dp'), split_axis=0, concat_axis=0, tiled=T...]
    ppermute x0 -> x3, starting transfers between devices: none -> 8.39 us  [move(): return lax.ppermute(x, ('seq', 'dp'), pairs)]
    pallas_call x7, Pallas kernels: 61.6 us -> 53.7 us  [the longest x1 22 us: mix(): pl.pallas_call(mix_kernel, in_specs=[smem, smem, whole, whole, whole], ou...]
  transfers between devices with their start and end apart: 2 -> 4, of which waited for: 1 -> 0; matrix products, arithmetic and copies ran while one was open for 0% -> 0% of each run, Pallas kernels for 6% -> 6%
where the time goes in v3:
time: 288 us; the launch traced here: 285 us
  blocking collectives  222 us (77%)
  Pallas kernels  53.7 us (19%)
  starting transfers between devices  8.48 us (3%)
    all_to_all x2, blocking collectives, swap(): return lax.all_to_all(x, 'seq', split_axis=0, concat_axis=0, tiled=True)  222 us
    pallas_call x1, Pallas kernels, mix(): pl.pallas_call(mix_kernel, in_specs=[smem, smem, whole, whole, whole], ou...  22 us
    pallas_call x1, Pallas kernels, gather(): pl.pallas_call(gather_kernel, grid=(channels // SUB,), in_specs=[pl.Block...  10.7 us
    pallas_call x1, Pallas kernels, spread(): pl.pallas_call(spread_kernel, grid=(channels // SUB,), in_specs=[smem] +...  9.71 us
    ppermute x3, starting transfers between devices, move(): return lax.ppermute(x, ('seq', 'dp'), pairs)  8.39 us
    pallas_call x1, Pallas kernels, back(): pl.pallas_call(lambda *refs: back_kernel(rows, *refs), grid=(2,), in_spec...  6.8 us
  transfers between devices with their start and end apart: 4, of which 0 were waited for; matrix products, arithmetic and copies ran while one was open for 0% of the time, Pallas kernels for 6%

profile of v3, /device:TPU:0, one launch (start us, length us, event | category | flops | bytes accessed | tf_op | source)
XLA Modules:
  0.0 284.8 jit_solution(15799766145454965981)
XLA Ops:
  0.6 0.1 pad_add_fusion.place_ref
  0.7 9.7 %shard_map.93 = (bf16[32,2,2,32,1024]{4,3,2,1,0:T(8,128)(2,1)}, s32[2]{0:T(128)S(1)}) custom-call(s32[2]{0:T(128)S(1)} %pad_add_fusion.place_ref, bf16[1,32,64,1024]{3,2,1,0:T(8,128)(2,1)} %x_ref.1, bf16[1,32,64,1024]{3,2,1,0:T(8,128)(2,1)} %cot_ref.3, bf16[1,32,64,1024]{3,2,1,0:T(8,128)(2,1)} %gate_ref.3), custom_call_target="tpu_custom_call" | custom-call | tf_op jit(solution)/shard_map/pallas_call | solution.py:62
  10.4 0.0 copy-start.2
  10.4 105.8 %all_to_all.10.in_hbm_ref = bf16[32,2,2,32,1024]{4,3,2,1,0:T(8,128)(2,1)} all-to-all(bf16[32,2,2,32,1024]{4,3,2,1,0:T(8,128)(2,1)} %get-tuple-element.18), channel_id=1, replica_groups=mesh['seq'=32,'dp'=4] {'seq'}, dimensions={0} | all-to-all | bytes 16777216 | tf_op jit(solution)/shard_map/all_to_all | solution.py:398
  116.3 0.0 copy-done.2
  116.3 22.0 %shard_map.94 = (bf16[32,73,16,128]{3,2,1,0:T(8,128)(2,1)}, bf16[2,1024,1024]{2,1,0:T(8,128)(2,1)}, bf16[1024,1024]{1,0:T(8,128)(2,1)}, f32[32,9,16,128]{3,2,1,0:T(8,128)}, bf16[32,9,16,128]{3,2,1,0:T(8,128)(2,1)}) custom-call(s32[2]{0:T(128)} %copy-done.2, s32[8,8]{1,0:T(8,128)} %refs_1_.1, bf16[1024,1024]{1,0:T(8,128)(2,1)} %left_hbm.1, ...), custom_call_target="tpu_custom_call" | custom-call | tf_op jit(solution)/shard_map/pallas_call | solution.py:241
  138.3 0.1 collective-permute-start
  138.3 0.0 copy-start
  138.4 6.8 %shard_map.95.parts_ref = bf16[32,73,16,128]{3,2,1,0:T(8,128)(2,1)} custom-call(bf16[1024,1024]{1,0:T(8,128)(2,1)} %get-tuple-element.21.refs_0_, bf16[2,1024,1024]{2,1,0:T(8,128)(2,1)} %get-tuple-element.22.refs_1_, bf16[32,73,16,128]{3,2,1,0:T(8,128)(2,1)} %get-tuple-element.23.refs_2_), custom_call_target="tpu_custom_call", output_to_operand_aliasing={{}: (2, {})} | custom-call | tf_op jit(solution)/shard_map/pallas_call | solution.py:286
  145.2 0.0 collective-permute-done.got_ref
  145.2 0.0 copy-done
  145.2 1.3 shard_map.96
  146.4 0.0 copy-start.3
  146.4 115.9 %all_to_all.11.parts_ref.in_ref = bf16[32,73,16,128]{3,2,1,0:T(8,128)(2,1)} all-to-all(bf16[32,73,16,128]{3,2,1,0:T(8,128)(2,1)} %shard_map.96), channel_id=1, replica_groups=mesh['seq'=32,'dp'=4] {'seq'}, dimensions={0} | all-to-all | bytes 19136512 | tf_op jit(solution)/shard_map/all_to_all | solution.py:398
  262.3 0.0 copy-done.3
  262.3 2.1 shard_map.97
  264.4 2.9 %collective-permute-start.3 = (f32[9,8,128]{2,1,0:T(8,128)S(1)}, f32[9,8,128]{2,1,0:T(8,128)S(1)}, u32[]{:S(2)}, u32[]{:S(2)}) collective-permute-start(f32[9,8,128]{2,1,0:T(8,128)S(1)} %get-tuple-element.27), channel_id=1, source_target_pairs={{0,126},{1,127},{2,124},{3,125},{4,122},{5,123},{6,120},{7,121},{8... | collective-permute-start | bytes 110600 | tf_op jit(solution)/shard_map/ppermute | solution.py:429
  267.3 0.6 collective-permute-start.1
  267.9 0.0 copy-start.1
  267.9 4.9 %collective-permute-start.2 = (f32[9,8,128]{2,1,0:T(8,128)S(1)}, f32[9,8,128]{2,1,0:T(8,128)S(1)}, u32[]{:S(2)}, u32[]{:S(2)}) collective-permute-start(f32[9,8,128]{2,1,0:T(8,128)S(1)} %get-tuple-element.24.after_ref.refs_2_), channel_id=1, source_target_pairs={{0,124},{1,125},{2,126},{3,127},{4,120},{5,121},{6,122},{7,123},{8... | collective-permute-start | bytes 110600 | tf_op jit(solution)/shard_map/ppermute | solution.py:429
  272.8 10.7 %shard_map.98 = (bf16[1,32,64,1024]{3,2,1,0:T(8,128)(2,1)}, bf16[1,32,64,1024]{3,2,1,0:T(8,128)(2,1)}) custom-call(bf16[32,73,16,128]{3,2,1,0:T(8,128)(2,1)} %all_to_all.11.parts_ref.in_ref, bf16[1,32,64,1024]{3,2,1,0:T(8,128)(2,1)} %cot_ref.3, bf16[1,32,64,1024]{3,2,1,0:T(8,128)(2,1)} %gate_ref.3, f32[9,8,128]{2,1,0:T(8,128)S(1)} %get-tuple-element.24.after_ref.refs_2_), custom_call_target="tpu_custom_call" | custom-call | tf_op jit(solution)/shard_map/pallas_call | solution.py:105
  283.5 0.0 collective-permute-done.3.refs_5_
  283.5 0.0 collective-permute-done.1.refs_3_
  283.5 0.0 collective-permute-done.2.refs_4_
  283.5 0.0 copy-done.1
  283.5 1.3 shard_map.99
Async XLA Ops:
  10.4 105.8 %copy-start.2 = (s32[2]{0:T(128)}, s32[2]{0:T(128)S(1)}, u32[]{:S(2)}) copy-start(s32[2]{0:T(128)S(1)} %get-tuple-element.17.place_ref.refs_0_) | copy-start | bytes 28
  138.3 6.9 %collective-permute-start = (bf16[32,9,16,128]{3,2,1,0:T(8,128)(2,1)}, bf16[32,9,16,128]{3,2,1,0:T(8,128)(2,1)S(1)}, u32[]{:S(2)}, u32[]{:S(2)}) collective-permute-start(bf16[32,9,16,128]{3,2,1,0:T(8,128)(2,1)} %get-tuple-element.20), channel_id=1, source_target_pairs={{0,1},{1,0},{2,3},{3,2},{4,5},{5,4},{6,7},{7,6},{8,9},{9,8},{10,11... | collective-permute-start | bytes 3538952 | tf_op jit(solution)/shard_map/ppermute | solution.py:414
  138.3 6.8 %copy-start = (f32[32,9,16,128]{3,2,1,0:T(8,128)S(1)}, f32[32,9,16,128]{3,2,1,0:T(8,128)}, u32[]{:S(2)}) copy-start(f32[32,9,16,128]{3,2,1,0:T(8,128)} %get-tuple-element.19.keep_ref) | copy-start | bytes 7077892
  146.4 115.9 %copy-start.3 = (s32[2]{0:T(128)S(1)}, s32[2]{0:T(128)}, u32[]{:S(2)}) copy-start(s32[2]{0:T(128)} %copy-done.2) | copy-start | bytes 28
  264.4 19.1 %collective-permute-start.3 = (f32[9,8,128]{2,1,0:T(8,128)S(1)}, f32[9,8,128]{2,1,0:T(8,128)S(1)}, u32[]{:S(2)}, u32[]{:S(2)}) collective-permute-start(f32[9,8,128]{2,1,0:T(8,128)S(1)} %get-tuple-element.27), channel_id=1, source_target_pairs={{0,126},{1,127},{2,124},{3,125},{4,122},{5,123},{6,120},{7,121},{8... | collective-permute-start | bytes 110600 | tf_op jit(solution)/shard_map/ppermute | solution.py:429
  267.3 16.2 %collective-permute-start.1 = (f32[9,8,128]{2,1,0:T(8,128)S(1)}, f32[9,8,128]{2,1,0:T(8,128)S(1)}, u32[]{:S(2)}, u32[]{:S(2)}) collective-permute-start(f32[9,8,128]{2,1,0:T(8,128)S(1)} %get-tuple-element.27), channel_id=1, source_target_pairs={{0,2},{1,3},{2,0},{3,1},{4,6},{5,7},{6,4},{7,5},{8,10},{9,11},{10,... | collective-permute-start | bytes 110600 | tf_op jit(solution)/shard_map/ppermute | solution.py:429
  267.9 15.6 %copy-start.1 = (s32[8,8]{1,0:T(8,128)S(1)}, s32[8,8]{1,0:T(8,128)}, u32[]{:S(2)}) copy-start(s32[8,8]{1,0:T(8,128)} %refs_1_.1) | copy-start | bytes 772
  267.9 15.6 %collective-permute-start.2 = (f32[9,8,128]{2,1,0:T(8,128)S(1)}, f32[9,8,128]{2,1,0:T(8,128)S(1)}, u32[]{:S(2)}, u32[]{:S(2)}) collective-permute-start(f32[9,8,128]{2,1,0:T(8,128)S(1)} %get-tuple-element.24.after_ref.refs_2_), channel_id=1, source_target_pairs={{0,124},{1,125},{2,126},{3,127},{4,120},{5,121},{6,122},{7,123},{8... | collective-permute-start | bytes 110600 | tf_op jit(solution)/shard_map/ppermute | solution.py:429

commit v4 on v0

v4 whole, which is shorter than its diff:
```python
import math

import jax
import jax.numpy as jnp
from jax import lax
from jax.experimental import pallas as pl
from jax.experimental.pallas import tpu as pltpu
from jax.sharding import PartitionSpec as P

BF = jnp.bfloat16
F32 = jnp.float32
MIB = 1024 * 1024
LANES = 128
SUB = 16
SIDE = 256


def params(mib):
    return pltpu.CompilerParams(vmem_limit_bytes=mib * MIB)


def shape(dims, dtype):
    return jax.ShapeDtypeStruct(dims, dtype)


def in_hbm(x):
    return pltpu.with_memory_space_constraint(x, pltpu.HBM)


def dot(a, b, on_a, on_b):
    return lax.dot_general(a, b, (((on_a,), (on_b,)), ((), ())), preferred_element_type=F32)


class Copies:
    def __init__(self, sems):
        self.sems, self.all, self.begun = sems, [], 0

    def add(self, src, dst):
        self.all.append(pltpu.make_async_copy(src, dst, self.sems.at[len(self.all)]))
        return len(self.all) - 1

    def begin(self, count):
        for copy in self.all[self.begun : count]:
            copy.start()
        self.begun = max(self.begun, min(count, len(self.all)))

    def start(self, src, dst):
        self.add(src, dst)
        self.begin(len(self.all))

    def take(self, index, ahead=0):
        self.begin(index + 1 + ahead)
        self.all[index].wait()

    def wait(self):
        for copy in self.all:
            copy.wait()


def put_tiles(ref, lead, part, rows, first_tile, tiles):
    devices, halves = part.shape[0] // rows, rows // SUB
    for tile in range(part.shape[1] // LANES):
        piece = part[:, tile * LANES : (tile + 1) * LANES].reshape(devices, halves, SUB, LANES)
        for half in range(halves):
            at = half * tiles + first_tile + tile
            ref[lead : lead + devices, at] = piece[:, half]


def turning():
    size = SUB * SUB
    row = lax.broadcasted_iota(jnp.int32, (size, size), 0)
    col = lax.broadcasted_iota(jnp.int32, (size, size), 1)
    return jnp.where(col == row % SUB * SUB + row // SUB, 1.0, 0.0).astype(BF)


def chunks_of(rows, channels):
    for group in range(channels // SUB):
        devices = pl.ds(group * SUB // 2, SUB // 2)
        for half in range(rows // SUB):
            yield half, pl.ds(half * SUB, SUB), pl.ds(group * SUB, SUB), devices


def spread_kernel(
    place_ref, x_hbm, cot_hbm, gate_hbm, out_hbm, place_out_ref,
    x, cot, gate, out, in_sems, out_sems,
):
    for k in range(place_ref.shape[0]):
        place_out_ref[k] = place_ref[k]
    _, rows, channels, width = x.shape
    size, dims = SUB * SUB, (SUB // 2, 2, SUB, width)
    loads, stores = Copies(in_sems), Copies(out_sems)
    chunks, turned = list(chunks_of(rows, channels)), turning()
    for _, at, group, _ in chunks:
        for src, dst in ((x_hbm, x), (cot_hbm, cot), (gate_hbm, gate)):
            loads.add(src.at[0, at, group], dst.at[0, at, group])
    loads.begin(len(loads.all))
    for k, (_, at, group, devices) in enumerate(chunks):
        for copy in range(3):
            loads.take(3 * k + copy)
        part = dot(turned, x[0, at, group].reshape(size, width), 1, 0)
        out[devices, :, 0, at] = part.astype(BF).reshape(dims)
        tanh = jnp.tanh(gate[0, at, group].astype(F32) * 0.5)
        grad = (cot[0, at, group].astype(F32) * (0.5 + 0.5 * tanh)).astype(BF)
        part = dot(turned, grad.reshape(size, width), 1, 0)
        out[devices, :, 1, at] = part.astype(BF).reshape(dims)
        stores.start(out.at[devices, :, :, at], out_hbm.at[devices, :, :, at])
    stores.wait()


def spread(place, x, cot, gate):
    _, rows, channels, width = x.shape
    smem = pl.BlockSpec(memory_space=pltpu.SMEM)
    whole = pl.BlockSpec(memory_space=pl.ANY)
    dims = (channels // 2, 2, 2, rows, width)
    count = rows * channels // (SUB * SUB)
    return pl.pallas_call(
        spread_kernel,
        in_specs=[smem] + [whole] * 3,
        out_specs=(whole, smem),
        out_shape=(pltpu.HBM(dims, BF), shape(place.shape, place.dtype)),
        scratch_shapes=[pltpu.VMEM(x.shape, BF)] * 3
        + [
            pltpu.VMEM(dims, BF),
            pltpu.SemaphoreType.DMA((3 * count,)),
            pltpu.SemaphoreType.DMA((count,)),
        ],
        compiler_params=params(48),
    )(place, in_hbm(x), in_hbm(cot), in_hbm(gate))


def gather_kernel(
    lead_hbm, in_hbm_ref, cot_hbm, gate_hbm, after_ref, back_hbm, grad_hbm,
    ahead, parts, cot, gate, back, grad, in_sems, out_sems,
):
    _, rows, channels, width = cot.shape
    size, dims = SUB * SUB, (SUB, SUB, width)
    tiles, halves = width // LANES, rows // SUB
    loads, stores = Copies(in_sems), Copies(out_sems)
    chunks, turned = list(chunks_of(rows, channels)), turning()

    def tiles_at(half, k):
        return pl.ds((k * halves + half) * tiles, tiles)

    for half, at, group, devices in chunks:
        where = (devices, tiles_at(half, 0))
        loads.add(lead_hbm.at[where], ahead.at[where])
        for k in range(3):
            where = (devices, tiles_at(half, k))
            loads.add(in_hbm_ref.at[where], parts.at[where])
        for src, dst in ((cot_hbm, cot), (gate_hbm, gate)):
            loads.add(src.at[0, at, group], dst.at[0, at, group])

    def rows_of(both, half, devices):
        columns = []
        for tile in range(tiles):
            pair = [ref[devices, (k * halves + half) * tiles + tile] for ref, k in both]
            columns.append(jnp.stack(pair, 1).reshape(size, LANES))
        return dot(turned, jnp.concatenate(columns, 1), 1, 0)

    loads.begin(len(loads.all))
    for k, (half, at, group, devices) in enumerate(chunks):
        for copy in range(6):
            loads.take(6 * k + copy)
        part = rows_of(((parts, 1), (parts, 2)), half, devices)
        back[0, at, group] = part.astype(BF).reshape(dims)
        stores.start(back.at[0, at, group], back_hbm.at[0, at, group])
        mixed = rows_of(((ahead, 0), (parts, 0)), half, devices).reshape(dims)
        tanh = jnp.tanh(gate[0, at, group].astype(F32) * 0.5)
        slope = 0.25 * (1.0 - tanh) * (1.0 + tanh)
        grad[0, at, group] = (cot[0, at, group].astype(F32) * mixed * slope).astype(BF)
        stores.start(grad.at[0, at, group], grad_hbm.at[0, at, group])
    stores.wait()


def gather(ahead, parts, cot, gate, after):
    _, rows, channels, width = cot.shape
    whole = pl.BlockSpec(memory_space=pl.ANY)
    devices, blocks = ahead.shape[:2]
    count = rows * channels // (SUB * SUB)
    natural = pltpu.VMEM(cot.shape, BF)
    return pl.pallas_call(
        gather_kernel,
        in_specs=[whole] * 5,
        out_specs=(whole, whole),
        out_shape=(pltpu.HBM(cot.shape, BF), pltpu.HBM(cot.shape, BF)),
        scratch_shapes=[
            pltpu.VMEM(ahead.shape, BF),
            pltpu.VMEM((devices, 3 * blocks, SUB, LANES), BF),
            natural,
            natural,
            natural,
            natural,
            pltpu.SemaphoreType.DMA((6 * count,)),
            pltpu.SemaphoreType.DMA((2 * count,)),
        ],
        compiler_params=params(48),
    )(in_hbm(ahead), in_hbm(parts), in_hbm(cot), in_hbm(gate), after)


def mask_factor(tiles_ref, ref, begin):
    count = tiles_ref.shape[0]
    side = ref.shape[0] // count
    for a in range(begin // side, (begin + SIDE) // side):
        for b in range((begin + SIDE) // side):
            where = (slice(a * side, (a + 1) * side), slice(b * side, (b + 1) * side))
            if b > a:
                ref[where] = jnp.zeros((side, side), BF)
            else:
                keep = jnp.full((side, side), tiles_ref[a, b].astype(F32)).astype(BF)
                ref[where] = ref[where] * keep


def blocks_of(width):
    return [(at, at + SIDE) for at in range(0, width, SIDE)]


def first_product(x, right, first):
    for at, end in blocks_of(x.shape[0]):
        first[:, at:end] = dot(x[:, :end], right[at:end, :end], 1, 1).astype(BF)


def mixed_product(left, first, mixed, rows):
    for at, end in blocks_of(left.shape[0]):
        part = dot(left[at:end, :end], first[:end], 1, 0).astype(BF)
        put_tiles(mixed, at // rows, part, rows, 0, part.shape[1] // LANES)


def lead_kernel(
    tiles_ref, left_hbm, right_hbm, parts_hbm, out_hbm, first_hbm,
    left, right, x, first, mixed, in_sems, out_sems,
):
    width, rows = left.shape[0], x.shape[1]
    blocks = blocks_of(width)
    loads, stores = Copies(in_sems), Copies(out_sems)

    count = len(blocks)

    def strip_of(src, dst, at, end):
        strip = (pl.ds(at, SIDE), pl.ds(0, end))
        loads.add(src.at[strip], dst.at[strip])

    for at, end in blocks:
        strip_of(right_hbm, right, at, end)
    for at, end in blocks:
        devices = pl.ds(at // rows, SIDE // rows)
        loads.add(parts_hbm.at[devices, 0, 0], x.at[devices])
    for at, end in blocks:
        strip_of(left_hbm, left, at, end)
    loads.begin(2 * count)
    for k, (at, _) in enumerate(blocks):
        loads.take(k)
        mask_factor(tiles_ref, right, at)
    loads.begin(3 * count)
    for k, (begin, stop) in enumerate(blocks):
        loads.take(count + k)
        strip = x[begin // rows : stop // rows].reshape(SIDE, width)
        for at, end in blocks:
            part = dot(strip[:, :end], right[at:end, :end], 1, 1)
            first[begin:stop, at:end] = part.astype(BF)
        stores.start(first.at[pl.ds(begin, SIDE)], first_hbm.at[pl.ds(begin, SIDE)])
    for k, (at, end) in enumerate(blocks):
        loads.take(2 * count + k)
        mask_factor(tiles_ref, left, at)
        part = dot(left[at:end, :end], first[:end], 1, 0).astype(BF)
        put_tiles(mixed, at // rows, part, rows, 0, width // LANES)
        devices = pl.ds(at // rows, SIDE // rows)
        stores.start(mixed.at[devices], out_hbm.at[devices])
    stores.wait()


def lead(tiles, left, right, parts):
    devices, _, _, rows, width = parts.shape
    whole = pl.BlockSpec(memory_space=pl.ANY)
    square = pltpu.VMEM((width, width), BF)
    dims = (devices, rows * width // (SUB * LANES), SUB, LANES)
    return pl.pallas_call(
        lead_kernel,
        in_specs=[pl.BlockSpec(memory_space=pltpu.SMEM), whole, whole, whole],
        out_specs=(whole, whole),
        out_shape=(pltpu.HBM(dims, BF), pltpu.HBM((width, width), BF)),
        scratch_shapes=[
            square,
            square,
            pltpu.VMEM((devices, rows, width), BF),
            square,
            pltpu.VMEM(dims, BF),
            pltpu.SemaphoreType.DMA((3 * width // SIDE,)),
            pltpu.SemaphoreType.DMA((2 * width // SIDE,)),
        ],
        compiler_params=params(32),
    )(tiles, in_hbm(left), in_hbm(right), in_hbm(parts))


def rest_kernel(
    place_ref, tiles_ref, left_hbm, right_hbm, parts_hbm, first_hbm,
    out_hbm, keep_hbm, give_hbm,
    left, right, xs, gs, first, grad, outs, total, keep, give, in_sems, out_sems,
):
    width, rows = left.shape[0], xs.shape[2]
    devices = width // rows
    loads, stores = Copies(in_sems), Copies(out_sems)
    blocks = blocks_of(width)
    for at, end in reversed(blocks):
        strip = (pl.ds(at, SIDE), pl.ds(0, end))
        loads.add(left_hbm.at[strip], left.at[strip])
        devices_at = pl.ds(at // rows, SIDE // rows)
        loads.add(parts_hbm.at[devices_at, 0, 1], gs.at[0, devices_at])
    strips = len(loads.all)
    loads.add(parts_hbm.at[:, 1, 1], gs.at[1])
    loads.add(right_hbm, right)
    loads.add(parts_hbm.at[:, 1, 0], xs.at[1])
    loads.add(first_hbm, first.at[0])
    loads.add(parts_hbm.at[:, 0, 0], xs.at[0])

    def send(k, begin=0, stop=devices):
        where, count = pl.ds(begin, stop - begin), outs.shape[2]
        stores.start(outs.at[k, where], out_hbm.at[where, pl.ds(k * count, count)])

    for c in range(2):
        loads.begin(strips + 2 * c + 1)
        if c == 1:
            loads.take(strips)
        for k, (at, end) in enumerate(reversed(blocks)):
            if c == 0:
                loads.take(2 * k)
                loads.take(2 * k + 1)
                mask_factor(tiles_ref, left, at)
            g = gs[c, at // rows :].reshape(width - at, width)
            grad[c, at:end] = dot(left[at:, at:end], g, 0, 0).astype(BF)
    loads.begin(len(loads.all))
    loads.take(strips + 1)
    for at, _ in blocks:
        mask_factor(tiles_ref, right, at)
    loads.take(strips + 2)
    first_product(xs[1].reshape(width, width), right, first.at[1])
    mixed_product(left, first.at[1], outs.at[0], rows)
    send(0)
    loads.take(strips + 3)
    loads.take(strips + 4)

    core = place_ref[0] % 2
    side = width // tiles_ref.shape[0]
    per_tile = devices * side // width
    for at, end in blocks_of(width):
        sums = [None, None]
        for c in range(2):
            x, g = xs[c].reshape(width, width), gs[c].reshape(width, width)
            left_part = dot(g[at:end], first[c, :end], 1, 1)
            right_part = dot(grad[c, :, at:end], x[:, :end], 0, 0)
            for k, part in enumerate((left_part, right_part)):
                sums[k] = part if sums[k] is None else sums[k] + part
        for k in range(2):
            total[k, :, :, :, :, :end] = sums[k].reshape(total.shape[1:5] + (end,))
        for s in range(at // rows, end // rows):
            lower = s < devices // 2
            mirror = devices - 1 - s
            first_tile = 0 if lower else (mirror // per_tile) + 1
            for k in range(2):
                to = (s if lower else mirror) if k == 0 else (mirror if lower else s)
                for tile in range(s // per_tile + 1):
                    cols = slice(tile * LANES, (tile + 1) * LANES)
                    place = first_tile + tile
                    own = total[k, s - at // rows, :, core, :, cols]
                    keep[to, place] = own.reshape(SUB, LANES)
                    other = total[k, s - at // rows, :, 1 - core, :, cols]
                    give[to, place] = other.reshape(SUB, LANES).astype(BF)
    stores.start(keep, keep_hbm)
    stores.start(give, give_hbm)

    for c in range(2):
        for begin, stop in blocks:
            for at, end in blocks:
                part = dot(grad[c, begin:stop, at:], right[at:, at:end], 1, 0).astype(BF)
                lead_device = begin // rows
                put_tiles(outs.at[1 + c], lead_device, part, rows, at // LANES, width // LANES)
            send(1 + c, begin // rows, stop // rows)
    stores.wait()


def rest(place, tiles, left, right, parts, first, own):
    devices, _, _, rows, width = parts.shape
    halves = rows // SUB
    count = width // LANES * halves
    terms = tiles.shape[0] + 1
    smem = pl.BlockSpec(memory_space=pltpu.SMEM)
    whole = pl.BlockSpec(memory_space=pl.ANY)
    square = pltpu.VMEM((width, width), BF)
    channels = pltpu.VMEM((2, devices, rows, width), BF)
    squares = pltpu.VMEM((2, width, width), BF)
    dims = (devices, terms, SUB, LANES)
    return pl.pallas_call(
        rest_kernel,
        in_specs=[smem, smem] + [whole] * 4,
        out_specs=(whole,) * 3,
        out_shape=(
            pltpu.HBM((devices, 3 * count + terms, SUB, LANES), BF),
            pltpu.HBM(dims, F32),
            pltpu.HBM(dims, BF),
        ),
        scratch_shapes=[
            square,
            square,
            channels,
            channels,
            squares,
            squares,
            pltpu.VMEM((3, devices, count, SUB, LANES), BF),
            pltpu.VMEM((2, SIDE // rows, halves, 2, own, width), F32),
            pltpu.VMEM(dims, F32),
            pltpu.VMEM(dims, BF),
            pltpu.SemaphoreType.DMA((5 + 2 * width // SIDE,)),
            pltpu.SemaphoreType.DMA((3 + 2 * width // SIDE,)),
        ],
        compiler_params=params(56),
    )(place, tiles, in_hbm(left), in_hbm(right), in_hbm(parts), in_hbm(first))


def add_kernel(keep_ref, got_ref, parts_ref, out_ref, total, sem):
    total[...] = (keep_ref[...] + got_ref[...].astype(F32)).astype(BF)
    terms = total.shape[1]
    copy = pltpu.make_async_copy(
        total, out_ref.at[:, pl.ds(out_ref.shape[1] - terms, terms)], sem
    )
    copy.start()
    copy.wait()


def add(keep, got, parts):
    vmem = pl.BlockSpec(memory_space=pltpu.VMEM)
    whole = pl.BlockSpec(memory_space=pl.ANY)
    return pl.pallas_call(
        add_kernel,
        in_specs=[vmem, vmem, whole],
        out_specs=whole,
        out_shape=pltpu.HBM(parts.shape, BF),
        input_output_aliases={2: 0},
        scratch_shapes=[pltpu.VMEM(keep.shape, BF), pltpu.SemaphoreType.DMA],
        compiler_params=params(16),
    )(keep, got, in_hbm(parts))


def tie_kernel(parts_ref, after_ref, out_ref):
    pass


def tie(parts, after):
    whole = pl.BlockSpec(memory_space=pl.ANY)
    return pl.pallas_call(
        tie_kernel,
        in_specs=[whole, whole],
        out_specs=whole,
        out_shape=pltpu.HBM(parts.shape, BF),
        input_output_aliases={0: 0},
    )(in_hbm(parts), after)


def fold_kernel(parts_ref, out_ref, got, sem):
    _, terms, own, _ = out_ref.shape
    copy = pltpu.make_async_copy(
        parts_ref.at[:, pl.ds(parts_ref.shape[1] - terms, terms)], got, sem
    )
    copy.start()
    copy.wait()
    total = jnp.sum(got[...].astype(F32), 0).reshape(terms, 2, own, LANES)
    for k in range(4):
        out_ref[k] = total[:, k % 2]


def fold(parts, terms, own):
    return pl.pallas_call(
        fold_kernel,
        in_specs=[pl.BlockSpec(memory_space=pl.ANY)],
        out_specs=pl.BlockSpec(memory_space=pltpu.VMEM),
        out_shape=shape((4, terms, own, LANES), F32),
        scratch_shapes=[
            pltpu.VMEM((parts.shape[0], terms, SUB, LANES), BF),
            pltpu.SemaphoreType.DMA,
        ],
        compiler_params=params(16),
    )(in_hbm(parts))


def finish_kernel(devices, scale, place_ref, tiles_ref, got_ref, left_ref, right_ref, total):
    count = tiles_ref.shape[0]
    total[0] = got_ref[0] + got_ref[1]
    total[1] = got_ref[2] + got_ref[3]
    row = place_ref[1] // (devices // count)
    start = jnp.where(place_ref[1] < devices // 2, 0, count - row)
    for tile in range(count):
        lanes = slice(tile * LANES, (tile + 1) * LANES)
        factor = tiles_ref[row, tile].astype(F32) * scale
        at = jnp.minimum(start + tile, count)
        left_ref[:, lanes] = total[0, at] * factor
        right_ref[:, lanes] = total[1, at] * factor


def finish(place, tiles, got, devices, scale):
    _, terms, own, _ = got.shape
    smem = pl.BlockSpec(memory_space=pltpu.SMEM)
    vmem = pl.BlockSpec(memory_space=pltpu.VMEM)
    out = shape((own, (terms - 1) * LANES), F32)
    return pl.pallas_call(
        lambda *refs: finish_kernel(devices, scale, *refs),
        in_specs=[smem, smem, vmem],
        out_specs=(vmem, vmem),
        out_shape=(out, out),
        scratch_shapes=[pltpu.VMEM((2, terms, own, LANES), F32)],
        compiler_params=params(16),
    )(place, tiles, got)


def swap(x):
    return lax.all_to_all(x, "seq", split_axis=0, concat_axis=0, tiled=True)


def shards(inputs, gate_in, cotangent, right_factor, left_factor, mask_tiles):
    width = right_factor.shape[0]
    rows, channels = inputs.shape[1], inputs.shape[2]
    seq_count = lax.axis_size("seq")
    data_count = lax.axis_size("dp")
    own = width // (seq_count * data_count)
    place = jnp.stack((lax.axis_index("dp"), lax.axis_index("seq"))).astype(jnp.int32)

    parts, place = spread(place, inputs, cotangent, gate_in)
    parts = swap(parts)
    ahead, first = lead(mask_tiles, left_factor, right_factor, parts)
    ahead = swap(ahead)
    parts, keep, give = rest(
        place, mask_tiles, left_factor, right_factor, parts, first, own
    )
    got = lax.ppermute(give, "dp", [(d, d ^ 1) for d in range(data_count)])
    parts = swap(tie(add(keep, got, parts), ahead))
    sums = fold(parts, mask_tiles.shape[0] + 1, own)
    groups = [
        [at * data_count + d for at in (s, seq_count - 1 - s) for d in (core, core + 2)]
        for s in range(seq_count // 2)
        for core in range(2)
    ]
    got = lax.all_to_all(
        sums,
        ("seq", "dp"),
        split_axis=0,
        concat_axis=0,
        tiled=True,
        axis_index_groups=groups,
    )
    grad_input, grad_gate = gather(ahead, parts, cotangent, gate_in, sums)
    scale = 1.0 / math.sqrt(data_count * channels * width)
    grad_left, grad_right = finish(place, mask_tiles, got, seq_count, scale)
    return grad_input, grad_gate, grad_right, grad_left


def solution(mesh):
    placed = (
        P("dp", "seq", None, None),
        P("dp", "seq", None, None),
        P("dp", "seq", None, None),
        P(),
        P(),
        P(),
    )
    return jax.shard_map(
        shards,
        mesh=mesh,
        in_specs=placed,
        out_specs=(
            P("dp", "seq", None, None),
            P("dp", "seq", None, None),
            P(("seq", "dp"), None),
            P(("seq", "dp"), None),
        ),
        check_vma=False,
    )
```

time: 1560 us -> 270 us (0.17)
  waiting for transfers between devices: 1240 us -> 6.79 us
  local copies, waits for them, and re-layouts: 58.6 us -> 3 us
  Pallas kernels: 0 us -> 52 us
  matrix products: 39.8 us -> 0 us
  blocking collectives: 171 us -> 198 us
  other arithmetic: 19.1 us -> 0.08 us
    reduce_scatter x2 -> x0, waiting for transfers between devices: 1200 us -> none  [reduce_factor(): lax.psum_scatter(term(jnp.int32(0), width // (seq_count * data_count) * l...]
    pallas_call x0 -> x8, Pallas kernels: none -> 52 us  [the longest x1 20.2 us: rest(): pl.pallas_call(rest_kernel, in_specs=[smem, smem] + [whole] * 4, out_spec...]
    all_to_all x1 -> x2, waiting for transfers between devices: 48.5 us -> 3.75 us  [the longest x1 3.75 us: swap(): return lax.all_to_all(x, 'seq', split_axis=0, concat_axis=0, tiled=True)]
    dot_general x6 -> x0, matrix products: 39.8 us -> none  [the longest x1 8.21 us: shards(): jnp.einsum('aick,kj->aicj', inner_piece, right_masked, preferred_element_...]
    all_to_all x3 -> x2, blocking collectives: 171 us -> 198 us  [swap(): return lax.all_to_all(x, 'seq', split_axis=0, concat_axis=0, tiled=True)]
    unnamed x34 -> x12, local copies, waits for them, and re-layouts: 29.3 us -> 3 us
    all_to_all x4 -> x0, local copies, waits for them, and re-layouts: 18.1 us -> none  [the longest x2 10.2 us: shards(): lax.all_to_all(grad_rows, 'seq', split_axis=1, concat_axis=0, tiled=True)]
    convert_element_type x2 -> x0, other arithmetic: 17.6 us -> none  [the longest x1 16.8 us: shards(): (cot_f * mixed_rows.astype(jnp.float32) * sig * (1.0 - sig)).astype(jnp.b...]
  transfers between devices with their start and end apart: 3 -> 3, of which waited for: 3 -> 2; matrix products, arithmetic and copies ran while one was open for 3% -> 0% of each run, Pallas kernels for 0% -> 12%
where the time goes in v4:
time: 270 us; the launch traced here: 269 us
  blocking collectives  198 us (73%)
  Pallas kernels  52 us (19%)
  starting transfers between devices  9.09 us (3%)
  waiting for transfers between devices  6.79 us (3%)
  local copies, waits for them, and re-layouts  3 us (1%)
    all_to_all x2, blocking collectives, swap(): return lax.all_to_all(x, 'seq', split_axis=0, concat_axis=0, tiled=True)  198 us
    pallas_call x1, Pallas kernels, rest(): pl.pallas_call(rest_kernel, in_specs=[smem, smem] + [whole] * 4, out_spec...  20.2 us
    pallas_call x1, Pallas kernels, gather(): pl.pallas_call(gather_kernel, in_specs=[whole] * 5, out_specs=(whole, who...  10 us
    pallas_call x1, Pallas kernels, spread(): pl.pallas_call(spread_kernel, in_specs=[smem] + [whole] * 3, out_specs=(w...  9.43 us
    pallas_call x1, Pallas kernels, lead(): pl.pallas_call(lead_kernel, in_specs=[pl.BlockSpec(memory_space=pltpu.SME...  7.76 us
  transfers between devices with their start and end apart: 3, of which 2 were waited for; matrix products, arithmetic and copies ran while one was open for 0% of the time, Pallas kernels for 12%

profile of v4, /device:TPU:0, one launch (start us, length us, event | category | flops | bytes accessed | tf_op | source)
XLA Modules:
  0.0 269.2 jit_solution(11770257061030226321)
XLA Ops:
  0.6 0.1 pad_add_fusion.place_ref
  0.7 9.4 %shard_map.93 = (bf16[32,2,2,32,1024]{4,3,2,1,0:T(8,128)(2,1)}, s32[2]{0:T(128)S(1)}) custom-call(s32[2]{0:T(128)S(1)} %pad_add_fusion.place_ref, bf16[1,32,64,1024]{3,2,1,0:T(8,128)(2,1)} %x_hbm.1, bf16[1,32,64,1024]{3,2,1,0:T(8,128)(2,1)} %cot_hbm.3, bf16[1,32,64,1024]{3,2,1,0:T(8,128)(2,1)} %gate_hbm.3), custom_call_target="tpu_custom_call" | custom-call | tf_op jit(solution)/shard_map/pallas_call | solution.py:116
  10.2 0.0 copy-start.3
  10.2 0.0 copy-start.1
  10.2 105.9 %all_to_all.20.parts_hbm = bf16[32,2,2,32,1024]{4,3,2,1,0:T(8,128)(2,1)} all-to-all(bf16[32,2,2,32,1024]{4,3,2,1,0:T(8,128)(2,1)} %get-tuple-element.15), channel_id=1, replica_groups=mesh['seq'=32,'dp'=4] {'seq'}, dimensions={0} | all-to-all | bytes 16777216 | tf_op jit(solution)/shard_map/all_to_all | solution.py:513
  116.1 0.0 copy-done.3
  116.1 0.0 copy-done.1
  116.1 7.8 %shard_map.94 = (bf16[32,16,16,128]{3,2,1,0:T(8,128)(2,1)}, bf16[1024,1024]{1,0:T(8,128)(2,1)}) custom-call(s32[8,8]{1,0:T(8,128)S(1)} %copy-done.1, bf16[1024,1024]{1,0:T(8,128)(2,1)} %left_hbm.3, bf16[1024,1024]{1,0:T(8,128)(2,1)} %right_hbm.3, bf16[32,2,2,32,1024]{4,3,2,1,0:T(8,128)(2,1)} %all_to_all.20.parts_hbm), custom_call_target="tpu_custom_call" | custom-call | tf_op jit(solution)/shard_map/pallas_call | solution.py:276
  123.9 4.3 %all-to-all-start.1 = ((bf16[32,16,16,128]{3,2,1,0:T(8,128)(2,1)}), bf16[32,16,16,128]{3,2,1,0:T(8,128)(2,1)S(1)}, u32[]{:S(2)}, u32[]{:S(2)}) async-start(bf16[32,16,16,128]{3,2,1,0:T(8,128)(2,1)} %get-tuple-element.16), calls=%async_computation.1 | async-start | bytes 4194304 | tf_op jit(solution)/shard_map/all_to_all | solution.py:513
  128.2 20.2 %shard_map.95 = (bf16[32,57,16,128]{3,2,1,0:T(8,128)(2,1)}, f32[32,9,16,128]{3,2,1,0:T(8,128)}, bf16[32,9,16,128]{3,2,1,0:T(8,128)(2,1)}) custom-call(s32[2]{0:T(128)} %copy-done.3, s32[8,8]{1,0:T(8,128)} %refs_1_.1, bf16[1024,1024]{1,0:T(8,128)(2,1)} %left_hbm.3, bf16[1024,1024]{1,0:T(8,128)(2,1)} %right_hbm.3, ...), custom_call_target="tpu_custom_call" | custom-call | tf_op jit(solution)/shard_map/pallas_call | solution.py:391
  148.3 0.1 collective-permute-start
  148.4 3.0 %collective-permute-done.got_ref = bf16[32,9,16,128]{3,2,1,0:T(8,128)(2,1)S(1)} collective-permute-done((bf16[32,9,16,128]{3,2,1,0:T(8,128)(2,1)}, bf16[32,9,16,128]{3,2,1,0:T(8,128)(2,1)S(1)}, u32[]{:S(2)}, u32[]{:S(2)}) %collective-permute-start) | collective-permute-done | bytes 1179680 | tf_op jit(solution)/shard_map/ppermute | solution.py:531
  151.5 0.0 copy-start
  151.5 1.7 copy-done
  153.1 1.2 shard_map.96.parts_ref
  154.4 3.7 %all-to-all-done.1.after_ref.lead_hbm = bf16[32,16,16,128]{3,2,1,0:T(8,128)(2,1)S(1)} async-done(((bf16[32,16,16,128]{3,2,1,0:T(8,128)(2,1)}), bf16[32,16,16,128]{3,2,1,0:T(8,128)(2,1)S(1)}, u32[]{:S(2)}, u32[]{:S(2)}) %all-to-all-start.1) | async-done | bytes 2097184 | tf_op jit(solution)/shard_map/all_to_all | solution.py:513
  158.1 0.0 copy-start.5
  158.1 1.3 copy-done.5
  159.4 91.6 %all_to_all.21.parts_ref.in_hbm_ref = bf16[32,57,16,128]{3,2,1,0:T(8,128)(2,1)} all-to-all(bf16[32,57,16,128]{3,2,1,0:T(8,128)(2,1)} %shard_map.97), channel_id=1, replica_groups=mesh['seq'=32,'dp'=4] {'seq'}, dimensions={0} | all-to-all | bytes 14942208 | tf_op jit(solution)/shard_map/all_to_all | solution.py:513
  251.0 2.1 shard_map.98.after_ref
  253.1 4.7 %all-to-all-start.3 = ((f32[4,9,8,128]{3,2,1,0:T(8,128)}), f32[4,9,8,128]{3,2,1,0:T(8,128)S(1)}, u32[]{:S(2)}, u32[]{:S(2)}) async-start(f32[4,9,8,128]{3,2,1,0:T(8,128)} %shard_map.98.after_ref), calls=%async_computation.3 | async-start | bytes 294912 | tf_op jit(solution)/shard_map/all_to_all | solution.py:539
  257.9 0.0 copy-start.2
  257.9 0.0 copy-start.4
  257.9 10.0 %shard_map.99 = (bf16[1,32,64,1024]{3,2,1,0:T(8,128)(2,1)}, bf16[1,32,64,1024]{3,2,1,0:T(8,128)(2,1)}) custom-call(bf16[32,16,16,128]{3,2,1,0:T(8,128)(2,1)} %copy-done.5, bf16[32,57,16,128]{3,2,1,0:T(8,128)(2,1)} %all_to_all.21.parts_ref.in_hbm_ref, bf16[1,32,64,1024]{3,2,1,0:T(8,128)(2,1)} %cot_hbm.3, bf16[1,32,64,1024]{3,2,1,0:T(8,128)(2,1)} %gate_hbm.3, ...), custom_call_target="tpu_custom_call" | custom-call | tf_op jit(solution)/shard_map/pallas_call | solution.py:181
  267.9 0.0 all-to-all-done.3.refs_2_
  267.9 0.0 copy-done.2
  267.9 0.0 copy-done.4
  267.9 1.3 shard_map.100
  (1 shorter events, 0.0 us)
Async XLA Ops:
  10.2 105.9 %copy-start.3 = (s32[2]{0:T(128)}, s32[2]{0:T(128)S(1)}, u32[]{:S(2)}) copy-start(s32[2]{0:T(128)S(1)} %get-tuple-element.17.place_ref.refs_0_) | copy-start | bytes 28
  10.2 105.9 %copy-start.1 = (s32[8,8]{1,0:T(8,128)S(1)}, s32[8,8]{1,0:T(8,128)}, u32[]{:S(2)}) copy-start(s32[8,8]{1,0:T(8,128)} %refs_1_.1) | copy-start | bytes 772
  123.9 34.2 %all-to-all-start.1 = ((bf16[32,16,16,128]{3,2,1,0:T(8,128)(2,1)}), bf16[32,16,16,128]{3,2,1,0:T(8,128)(2,1)S(1)}, u32[]{:S(2)}, u32[]{:S(2)}) async-start(bf16[32,16,16,128]{3,2,1,0:T(8,128)(2,1)} %get-tuple-element.16), calls=%async_computation.1 | async-start | bytes 4194304 | tf_op jit(solution)/shard_map/all_to_all | solution.py:513
  148.3 3.1 %collective-permute-start = (bf16[32,9,16,128]{3,2,1,0:T(8,128)(2,1)}, bf16[32,9,16,128]{3,2,1,0:T(8,128)(2,1)S(1)}, u32[]{:S(2)}, u32[]{:S(2)}) collective-permute-start(bf16[32,9,16,128]{3,2,1,0:T(8,128)(2,1)} %get-tuple-element.20), channel_id=1, source_target_pairs={{0,1},{1,0},{2,3},{3,2},{4,5},{5,4},{6,7},{7,6},{8,9},{9,8},{10,11... | collective-permute-start | bytes 3538952 | tf_op jit(solution)/shard_map/ppermute | solution.py:531
  151.5 1.7 copy-start
  158.1 1.3 copy-start.5
  253.1 14.8 %all-to-all-start.3 = ((f32[4,9,8,128]{3,2,1,0:T(8,128)}), f32[4,9,8,128]{3,2,1,0:T(8,128)S(1)}, u32[]{:S(2)}, u32[]{:S(2)}) async-start(f32[4,9,8,128]{3,2,1,0:T(8,128)} %shard_map.98.after_ref), calls=%async_computation.3 | async-start | bytes 294912 | tf_op jit(solution)/shard_map/all_to_all | solution.py:539
  257.9 10.1 %copy-start.2 = (s32[8,8]{1,0:T(8,128)S(1)}, s32[8,8]{1,0:T(8,128)}, u32[]{:S(2)}) copy-start(s32[8,8]{1,0:T(8,128)} %refs_1_.1) | copy-start | bytes 772
  257.9 10.1 %copy-start.4 = (s32[2]{0:T(128)S(1)}, s32[2]{0:T(128)}, u32[]{:S(2)}) copy-start(s32[2]{0:T(128)} %copy-done.3) | copy-start | bytes 28

commit v5 on v4

--- a/solution.py
+++ b/solution.py
@@ -194,7 +194,7 @@
             pltpu.SemaphoreType.DMA((2 * count,)),
         ],
         compiler_params=params(48),
-    )(in_hbm(ahead), in_hbm(parts), in_hbm(cot), in_hbm(gate), after)
+    )(ahead, in_hbm(parts), cot, gate, after)
 
 
 def mask_factor(tiles_ref, ref, begin):
@@ -288,13 +288,13 @@
             pltpu.SemaphoreType.DMA((2 * width // SIDE,)),
         ],
         compiler_params=params(32),
-    )(tiles, in_hbm(left), in_hbm(right), in_hbm(parts))
+    )(tiles, left, right, in_hbm(parts))
 
 
 def rest_kernel(
     place_ref, tiles_ref, left_hbm, right_hbm, parts_hbm, first_hbm,
-    out_hbm, keep_hbm, give_hbm,
-    left, right, xs, gs, first, grad, outs, total, keep, give, in_sems, out_sems,
+    out_hbm, keep, give,
+    left, right, xs, gs, first, grad, outs, total, in_sems, out_sems,
 ):
     width, rows = left.shape[0], xs.shape[2]
     devices = width // rows
@@ -364,8 +364,6 @@
                     keep[to, place] = own.reshape(SUB, LANES)
                     other = total[k, s - at // rows, :, 1 - core, :, cols]
                     give[to, place] = other.reshape(SUB, LANES).astype(BF)
-    stores.start(keep, keep_hbm)
-    stores.start(give, give_hbm)
 
     for c in range(2):
         for begin, stop in blocks:
@@ -384,6 +382,7 @@
     terms = tiles.shape[0] + 1
     smem = pl.BlockSpec(memory_space=pltpu.SMEM)
     whole = pl.BlockSpec(memory_space=pl.ANY)
+    vmem = pl.BlockSpec(memory_space=pltpu.VMEM)
     square = pltpu.VMEM((width, width), BF)
     channels = pltpu.VMEM((2, devices, rows, width), BF)
     squares = pltpu.VMEM((2, width, width), BF)
@@ -391,11 +390,11 @@
     return pl.pallas_call(
         rest_kernel,
         in_specs=[smem, smem] + [whole] * 4,
-        out_specs=(whole,) * 3,
+        out_specs=(whole, vmem, vmem),
         out_shape=(
             pltpu.HBM((devices, 3 * count + terms, SUB, LANES), BF),
-            pltpu.HBM(dims, F32),
-            pltpu.HBM(dims, BF),
+            pltpu.VMEM(dims, F32),
+            pltpu.VMEM(dims, BF),
         ),
         scratch_shapes=[
             square,
@@ -406,10 +405,8 @@
             squares,
             pltpu.VMEM((3, devices, count, SUB, LANES), BF),
             pltpu.VMEM((2, SIDE // rows, halves, 2, own, width), F32),
-            pltpu.VMEM(dims, F32),
-            pltpu.VMEM(dims, BF),
             pltpu.SemaphoreType.DMA((5 + 2 * width // SIDE,)),
-            pltpu.SemaphoreType.DMA((3 + 2 * width // SIDE,)),
+            pltpu.SemaphoreType.DMA((1 + 2 * width // SIDE,)),
         ],
         compiler_params=params(56),
     )(place, tiles, in_hbm(left), in_hbm(right), in_hbm(parts), in_hbm(first))
@@ -529,7 +526,7 @@
         place, mask_tiles, left_factor, right_factor, parts, first, own
     )
     got = lax.ppermute(give, "dp", [(d, d ^ 1) for d in range(data_count)])
-    parts = swap(tie(add(keep, got, parts), ahead))
+    parts = swap(tie(add(keep, got, parts), ahead[0, 0]))
     sums = fold(parts, mask_tiles.shape[0] + 1, own)
     groups = [
         [at * data_count + d for at in (s, seq_count - 1 - s) for d in (core, core + 2)]

time: 270 us -> 267 us (0.989)
    unnamed x12, local copies, waits for them, and re-layouts: 3 us -> 0.03 us
  transfers between devices with their start and end apart: 3 -> 3, of which waited for: 2 -> 3; matrix products, arithmetic and copies ran while one was open for 0% -> 0% of each run, Pallas kernels for 12% -> 12%
where the time goes in v5:
time: 267 us
  blocking collectives  196 us (73%)
  Pallas kernels  51 us (19%)
  starting transfers between devices  9.09 us (3%)
  waiting for transfers between devices  8.63 us (3%)
    all_to_all x2, blocking collectives, swap(): return lax.all_to_all(x, 'seq', split_axis=0, concat_axis=0, tiled=True)  196 us
    pallas_call x1, Pallas kernels, rest(): pl.pallas_call(rest_kernel, in_specs=[smem, smem] + [whole] * 4, out_spec...  20.1 us
    pallas_call x1, Pallas kernels, gather(): pl.pallas_call(gather_kernel, in_specs=[whole] * 5, out_specs=(whole, who...  9.49 us
    pallas_call x1, Pallas kernels, spread(): pl.pallas_call(spread_kernel, in_specs=[smem] + [whole] * 3, out_specs=(w...  9.43 us
    pallas_call x1, Pallas kernels, lead(): pl.pallas_call(lead_kernel, in_specs=[pl.BlockSpec(memory_space=pltpu.SME...  7.44 us
    all_to_all x1, waiting for transfers between devices, swap(): return lax.all_to_all(x, 'seq', split_axis=0, concat_axis=0, tiled=True)  5.7 us
  transfers between devices with their start and end apart: 3, of which 3 were waited for; matrix products, arithmetic and copies ran while one was open for 0% of the time, Pallas kernels for 12%

profile of v5, /device:TPU:0, one launch (start us, length us, event | category | flops | bytes accessed | tf_op | source)
XLA Modules:
  0.0 266.6 jit_solution(12892134779377052808)
XLA Ops:
  0.6 0.1 pad_add_fusion.place_ref
  0.7 9.4 %shard_map.93 = (bf16[32,2,2,32,1024]{4,3,2,1,0:T(8,128)(2,1)}, s32[2]{0:T(128)S(1)}) custom-call(s32[2]{0:T(128)S(1)} %pad_add_fusion.place_ref, bf16[1,32,64,1024]{3,2,1,0:T(8,128)(2,1)} %x_hbm.1, bf16[1,32,64,1024]{3,2,1,0:T(8,128)(2,1)} %cot_hbm.3, bf16[1,32,64,1024]{3,2,1,0:T(8,128)(2,1)} %gate_hbm.3), custom_call_target="tpu_custom_call" | custom-call | tf_op jit(solution)/shard_map/pallas_call | solution.py:116
  10.2 0.0 copy-start.4
  10.2 0.0 copy-start
  10.2 0.0 copy-start.1
  10.2 0.0 copy-start.2
  10.2 106.2 %all_to_all.20.parts_hbm = bf16[32,2,2,32,1024]{4,3,2,1,0:T(8,128)(2,1)} all-to-all(bf16[32,2,2,32,1024]{4,3,2,1,0:T(8,128)(2,1)} %get-tuple-element.15), channel_id=1, replica_groups=mesh['seq'=32,'dp'=4] {'seq'}, dimensions={0} | all-to-all | bytes 16777216 | tf_op jit(solution)/shard_map/all_to_all | solution.py:510
  116.4 0.0 copy-done.4
  116.4 0.0 copy-done
  116.4 0.0 copy-done.1
  116.4 0.0 copy-done.2
  116.4 7.4 %shard_map.94 = (bf16[32,16,16,128]{3,2,1,0:T(8,128)(2,1)}, bf16[1024,1024]{1,0:T(8,128)(2,1)}) custom-call(s32[8,8]{1,0:T(8,128)S(1)} %copy-done.2, bf16[1024,1024]{1,0:T(8,128)(2,1)S(1)} %copy-done, bf16[1024,1024]{1,0:T(8,128)(2,1)S(1)} %copy-done.1, bf16[32,2,2,32,1024]{4,3,2,1,0:T(8,128)(2,1)} %all_to_all.20.parts_hbm), custom_call_target="tpu_custom_call" | custom-call | tf_op jit(solution)/shard_map/pallas_call | solution.py:276
  123.8 4.3 %all-to-all-start.1 = ((bf16[32,16,16,128]{3,2,1,0:T(8,128)(2,1)}), bf16[32,16,16,128]{3,2,1,0:T(8,128)(2,1)S(1)}, u32[]{:S(2)}, u32[]{:S(2)}) async-start(bf16[32,16,16,128]{3,2,1,0:T(8,128)(2,1)} %get-tuple-element.16), calls=%async_computation.1 | async-start | bytes 4194304 | tf_op jit(solution)/shard_map/all_to_all | solution.py:510
  128.1 20.1 %shard_map.95 = (bf16[32,57,16,128]{3,2,1,0:T(8,128)(2,1)}, f32[32,9,16,128]{3,2,1,0:T(8,128)S(1)}, bf16[32,9,16,128]{3,2,1,0:T(8,128)(2,1)S(1)}) custom-call(s32[2]{0:T(128)} %copy-done.4, s32[8,8]{1,0:T(8,128)} %refs_1_.1, bf16[1024,1024]{1,0:T(8,128)(2,1)} %left_hbm.3, bf16[1024,1024]{1,0:T(8,128)(2,1)} %right_hbm.3, ...), custom_call_target="tpu_custom_call" | custom-call | tf_op jit(solution)/shard_map/pallas_call | solution.py:390
  148.2 0.1 collective-permute-start
  148.3 2.8 %collective-permute-done.got_ref = bf16[32,9,16,128]{3,2,1,0:T(8,128)(2,1)S(1)} collective-permute-done((bf16[32,9,16,128]{3,2,1,0:T(8,128)(2,1)S(1)}, bf16[32,9,16,128]{3,2,1,0:T(8,128)(2,1)S(1)}, u32[]{:S(2)}, u32[]{:S(2)}) %collective-permute-start) | collective-permute-done | bytes 1179680 | tf_op jit(solution)/shard_map/ppermute | solution.py:528
  151.1 1.2 shard_map.96.parts_ref
  152.4 5.7 %all-to-all-done.1.lead_hbm = bf16[32,16,16,128]{3,2,1,0:T(8,128)(2,1)S(1)} async-done(((bf16[32,16,16,128]{3,2,1,0:T(8,128)(2,1)}), bf16[32,16,16,128]{3,2,1,0:T(8,128)(2,1)S(1)}, u32[]{:S(2)}, u32[]{:S(2)}) %all-to-all-start.1) | async-done | bytes 2097184 | tf_op jit(solution)/shard_map/all_to_all | solution.py:510
  158.1 0.6 slice_bitcast_fusion.after_ref
  158.7 90.2 %all_to_all.21.parts_ref.in_hbm_ref = bf16[32,57,16,128]{3,2,1,0:T(8,128)(2,1)} all-to-all(bf16[32,57,16,128]{3,2,1,0:T(8,128)(2,1)} %shard_map.97), channel_id=1, replica_groups=mesh['seq'=32,'dp'=4] {'seq'}, dimensions={0} | all-to-all | bytes 14942208 | tf_op jit(solution)/shard_map/all_to_all | solution.py:510
  248.9 2.1 shard_map.98.after_ref
  251.0 4.7 %all-to-all-start.3 = ((f32[4,9,8,128]{3,2,1,0:T(8,128)}), f32[4,9,8,128]{3,2,1,0:T(8,128)S(1)}, u32[]{:S(2)}, u32[]{:S(2)}) async-start(f32[4,9,8,128]{3,2,1,0:T(8,128)} %shard_map.98.after_ref), calls=%async_computation.3 | async-start | bytes 294912 | tf_op jit(solution)/shard_map/all_to_all | solution.py:536
  255.7 0.0 copy-start.3
  255.7 0.0 copy-start.5
  255.7 9.5 %shard_map.99 = (bf16[1,32,64,1024]{3,2,1,0:T(8,128)(2,1)}, bf16[1,32,64,1024]{3,2,1,0:T(8,128)(2,1)}) custom-call(bf16[32,16,16,128]{3,2,1,0:T(8,128)(2,1)S(1)} %all-to-all-done.1.lead_hbm, bf16[32,57,16,128]{3,2,1,0:T(8,128)(2,1)} %all_to_all.21.parts_ref.in_hbm_ref, bf16[1,32,64,1024]{3,2,1,0:T(8,128)(2,1)} %cot_hbm.3, ...), custom_call_target="tpu_custom_call" | custom-call | tf_op jit(solution)/shard_map/pallas_call | solution.py:181
  265.2 0.1 all-to-all-done.3.refs_2_
  265.3 0.0 copy-done.3
  265.3 0.0 copy-done.5
  265.3 1.3 shard_map.100
  (1 shorter events, 0.0 us)
Async XLA Ops:
  10.2 106.2 %copy-start.4 = (s32[2]{0:T(128)}, s32[2]{0:T(128)S(1)}, u32[]{:S(2)}) copy-start(s32[2]{0:T(128)S(1)} %get-tuple-element.17.place_ref.refs_0_) | copy-start | bytes 28
  10.2 106.2 %copy-start = (bf16[1024,1024]{1,0:T(8,128)(2,1)S(1)}, bf16[1024,1024]{1,0:T(8,128)(2,1)}, u32[]{:S(2)}) copy-start(bf16[1024,1024]{1,0:T(8,128)(2,1)} %left_hbm.3) | copy-start | bytes 6291460
  10.2 106.2 %copy-start.1 = (bf16[1024,1024]{1,0:T(8,128)(2,1)S(1)}, bf16[1024,1024]{1,0:T(8,128)(2,1)}, u32[]{:S(2)}) copy-start(bf16[1024,1024]{1,0:T(8,128)(2,1)} %right_hbm.3) | copy-start | bytes 6291460
  10.2 106.2 %copy-start.2 = (s32[8,8]{1,0:T(8,128)S(1)}, s32[8,8]{1,0:T(8,128)}, u32[]{:S(2)}) copy-start(s32[8,8]{1,0:T(8,128)} %refs_1_.1) | copy-start | bytes 772
  123.8 34.2 %all-to-all-start.1 = ((bf16[32,16,16,128]{3,2,1,0:T(8,128)(2,1)}), bf16[32,16,16,128]{3,2,1,0:T(8,128)(2,1)S(1)}, u32[]{:S(2)}, u32[]{:S(2)}) async-start(bf16[32,16,16,128]{3,2,1,0:T(8,128)(2,1)} %get-tuple-element.16), calls=%async_computation.1 | async-start | bytes 4194304 | tf_op jit(solution)/shard_map/all_to_all | solution.py:510
  148.2 2.9 %collective-permute-start = (bf16[32,9,16,128]{3,2,1,0:T(8,128)(2,1)S(1)}, bf16[32,9,16,128]{3,2,1,0:T(8,128)(2,1)S(1)}, u32[]{:S(2)}, u32[]{:S(2)}) collective-permute-start(bf16[32,9,16,128]{3,2,1,0:T(8,128)(2,1)S(1)} %get-tuple-element.20), channel_id=1, source_target_pairs={{0,1},{1,0},{2,3},{3,2},{4,5},{5,4},{6,7},{7,6},{8,9},{9,8},{10,11... | collective-permute-start | bytes 3538952 | tf_op jit(solution)/shard_map/ppermute | solution.py:528
  251.0 14.3 %all-to-all-start.3 = ((f32[4,9,8,128]{3,2,1,0:T(8,128)}), f32[4,9,8,128]{3,2,1,0:T(8,128)S(1)}, u32[]{:S(2)}, u32[]{:S(2)}) async-start(f32[4,9,8,128]{3,2,1,0:T(8,128)} %shard_map.98.after_ref), calls=%async_computation.3 | async-start | bytes 294912 | tf_op jit(solution)/shard_map/all_to_all | solution.py:536
  255.7 9.6 %copy-start.3 = (s32[8,8]{1,0:T(8,128)S(1)}, s32[8,8]{1,0:T(8,128)}, u32[]{:S(2)}) copy-start(s32[8,8]{1,0:T(8,128)} %refs_1_.1) | copy-start | bytes 772
  255.7 9.6 %copy-start.5 = (s32[2]{0:T(128)S(1)}, s32[2]{0:T(128)}, u32[]{:S(2)}) copy-start(s32[2]{0:T(128)} %copy-done.4) | copy-start | bytes 28

commit v6 on v5

--- a/solution.py
+++ b/solution.py
@@ -81,30 +81,35 @@
 
 
 def spread_kernel(
-    place_ref, x_hbm, cot_hbm, gate_hbm, out_hbm, place_out_ref,
-    x, cot, gate, out, in_sems, out_sems,
+    place_ref, x_hbm, cot_hbm, gate_hbm, out, place_out_ref,
+    x, cot, gate, in_sems,
 ):
     for k in range(place_ref.shape[0]):
         place_out_ref[k] = place_ref[k]
     _, rows, channels, width = x.shape
     size, dims = SUB * SUB, (SUB // 2, 2, SUB, width)
-    loads, stores = Copies(in_sems), Copies(out_sems)
+    loads = Copies(in_sems)
     chunks, turned = list(chunks_of(rows, channels)), turning()
     for _, at, group, _ in chunks:
-        for src, dst in ((x_hbm, x), (cot_hbm, cot), (gate_hbm, gate)):
+        loads.add(x_hbm.at[0, at, group], x.at[0, at, group])
+    for _, at, group, _ in chunks:
+        for src, dst in ((cot_hbm, cot), (gate_hbm, gate)):
             loads.add(src.at[0, at, group], dst.at[0, at, group])
+    count = len(chunks)
+    loads.begin(count + 4)
+    for k, (_, at, group, devices) in enumerate(chunks):
+        loads.take(k)
+        loads.begin(count + 6 + 2 * k)
+        part = dot(turned, x[0, at, group].reshape(size, width), 1, 0)
+        out[devices, :, 0, at] = part.astype(BF).reshape(dims)
     loads.begin(len(loads.all))
     for k, (_, at, group, devices) in enumerate(chunks):
-        for copy in range(3):
-            loads.take(3 * k + copy)
-        part = dot(turned, x[0, at, group].reshape(size, width), 1, 0)
-        out[devices, :, 0, at] = part.astype(BF).reshape(dims)
+        for copy in range(2):
+            loads.take(count + 2 * k + copy)
         tanh = jnp.tanh(gate[0, at, group].astype(F32) * 0.5)
         grad = (cot[0, at, group].astype(F32) * (0.5 + 0.5 * tanh)).astype(BF)
         part = dot(turned, grad.reshape(size, width), 1, 0)
         out[devices, :, 1, at] = part.astype(BF).reshape(dims)
-        stores.start(out.at[devices, :, :, at], out_hbm.at[devices, :, :, at])
-    stores.wait()
 
 
 def spread(place, x, cot, gate):
@@ -116,14 +121,9 @@
     return pl.pallas_call(
         spread_kernel,
         in_specs=[smem] + [whole] * 3,
-        out_specs=(whole, smem),
-        out_shape=(pltpu.HBM(dims, BF), shape(place.shape, place.dtype)),
-        scratch_shapes=[pltpu.VMEM(x.shape, BF)] * 3
-        + [
-            pltpu.VMEM(dims, BF),
-            pltpu.SemaphoreType.DMA((3 * count,)),
-            pltpu.SemaphoreType.DMA((count,)),
-        ],
+        out_specs=(pl.BlockSpec(memory_space=pltpu.VMEM), smem),
+        out_shape=(pltpu.VMEM(dims, BF), shape(place.shape, place.dtype)),
+        scratch_shapes=[pltpu.VMEM(x.shape, BF)] * 3 + [pltpu.SemaphoreType.DMA((3 * count,))],
         compiler_params=params(48),
     )(place, in_hbm(x), in_hbm(cot), in_hbm(gate))
 

time: 267 us -> 267 us (level)
  no operation moved by 1% of the time
where the time goes in v6:
time: 267 us; the launch traced here: 266 us
  blocking collectives  196 us (73%)
  Pallas kernels  49.9 us (19%)
  starting transfers between devices  9.09 us (3%)
  waiting for transfers between devices  8.63 us (3%)
    all_to_all x2, blocking collectives, swap(): return lax.all_to_all(x, 'seq', split_axis=0, concat_axis=0, tiled=True)  196 us
    pallas_call x1, Pallas kernels, rest(): pl.pallas_call(rest_kernel, in_specs=[smem, smem] + [whole] * 4, out_spec...  20.1 us
    pallas_call x1, Pallas kernels, gather(): pl.pallas_call(gather_kernel, in_specs=[whole] * 5, out_specs=(whole, who...  9.49 us
    pallas_call x1, Pallas kernels, spread(): pl.pallas_call(spread_kernel, in_specs=[smem] + [whole] * 3, out_specs=(p...  8.31 us
    pallas_call x1, Pallas kernels, lead(): pl.pallas_call(lead_kernel, in_specs=[pl.BlockSpec(memory_space=pltpu.SME...  7.44 us
    all_to_all x1, waiting for transfers between devices, swap(): return lax.all_to_all(x, 'seq', split_axis=0, concat_axis=0, tiled=True)  5.7 us
  transfers between devices with their start and end apart: 3, of which 3 were waited for; matrix products, arithmetic and copies ran while one was open for 0% of the time, Pallas kernels for 12%

profile of v6, /device:TPU:0, one launch (start us, length us, event | category | flops | bytes accessed | tf_op | source)
XLA Modules:
  0.0 265.7 jit_solution(3574530037318721959)
XLA Ops:
  0.6 0.6 pad_add_fusion.place_ref
  1.2 8.3 %shard_map.93 = (bf16[32,2,2,32,1024]{4,3,2,1,0:T(8,128)(2,1)S(1)}, s32[2]{0:T(128)}) custom-call(s32[2]{0:T(128)} %pad_add_fusion.place_ref, bf16[1,32,64,1024]{3,2,1,0:T(8,128)(2,1)} %x_hbm.1, bf16[1,32,64,1024]{3,2,1,0:T(8,128)(2,1)} %cot_hbm.3, bf16[1,32,64,1024]{3,2,1,0:T(8,128)(2,1)} %gate_hbm.3), custom_call_target="tpu_custom_call" | custom-call | tf_op jit(solution)/shard_map/pallas_call | solution.py:121
  9.5 0.0 copy-start
  9.6 0.0 copy-start.1
  9.6 0.0 copy-start.2
  9.6 105.9 %all_to_all.20.parts_hbm = bf16[32,2,2,32,1024]{4,3,2,1,0:T(8,128)(2,1)} all-to-all(bf16[32,2,2,32,1024]{4,3,2,1,0:T(8,128)(2,1)S(1)} %get-tuple-element.15), channel_id=1, replica_groups=mesh['seq'=32,'dp'=4] {'seq'}, dimensions={0} | all-to-all | bytes 16777216 | tf_op jit(solution)/shard_map/all_to_all | solution.py:510
  115.5 0.0 copy-done
  115.5 0.0 copy-done.1
  115.5 0.0 copy-done.2
  115.5 7.4 %shard_map.94 = (bf16[32,16,16,128]{3,2,1,0:T(8,128)(2,1)}, bf16[1024,1024]{1,0:T(8,128)(2,1)}) custom-call(s32[8,8]{1,0:T(8,128)S(1)} %copy-done.2, bf16[1024,1024]{1,0:T(8,128)(2,1)S(1)} %copy-done, bf16[1024,1024]{1,0:T(8,128)(2,1)S(1)} %copy-done.1, bf16[32,2,2,32,1024]{4,3,2,1,0:T(8,128)(2,1)} %all_to_all.20.parts_hbm), custom_call_target="tpu_custom_call" | custom-call | tf_op jit(solution)/shard_map/pallas_call | solution.py:276
  122.9 4.3 %all-to-all-start.1 = ((bf16[32,16,16,128]{3,2,1,0:T(8,128)(2,1)}), bf16[32,16,16,128]{3,2,1,0:T(8,128)(2,1)S(1)}, u32[]{:S(2)}, u32[]{:S(2)}) async-start(bf16[32,16,16,128]{3,2,1,0:T(8,128)(2,1)} %get-tuple-element.16), calls=%async_computation.1 | async-start | bytes 4194304 | tf_op jit(solution)/shard_map/all_to_all | solution.py:510
  127.3 20.1 %shard_map.95 = (bf16[32,57,16,128]{3,2,1,0:T(8,128)(2,1)}, f32[32,9,16,128]{3,2,1,0:T(8,128)S(1)}, bf16[32,9,16,128]{3,2,1,0:T(8,128)(2,1)S(1)}) custom-call(s32[2]{0:T(128)} %get-tuple-element.17.place_ref.refs_0_, s32[8,8]{1,0:T(8,128)} %refs_1_.1, bf16[1024,1024]{1,0:T(8,128)(2,1)} %left_hbm.3, bf16[1024,1024]{1,0:T(8,128)(2,1)} %right_hbm.3, ...), custom_call_target="tpu_custom_call" | custom-call | tf_op jit(solution)/shard_map/pallas_call | solution.py:390
  147.3 0.1 collective-permute-start
  147.4 2.8 %collective-permute-done.got_ref = bf16[32,9,16,128]{3,2,1,0:T(8,128)(2,1)S(1)} collective-permute-done((bf16[32,9,16,128]{3,2,1,0:T(8,128)(2,1)S(1)}, bf16[32,9,16,128]{3,2,1,0:T(8,128)(2,1)S(1)}, u32[]{:S(2)}, u32[]{:S(2)}) %collective-permute-start) | collective-permute-done | bytes 1179680 | tf_op jit(solution)/shard_map/ppermute | solution.py:528
  150.3 1.2 shard_map.96.parts_ref
  151.5 5.7 %all-to-all-done.1.lead_hbm = bf16[32,16,16,128]{3,2,1,0:T(8,128)(2,1)S(1)} async-done(((bf16[32,16,16,128]{3,2,1,0:T(8,128)(2,1)}), bf16[32,16,16,128]{3,2,1,0:T(8,128)(2,1)S(1)}, u32[]{:S(2)}, u32[]{:S(2)}) %all-to-all-start.1) | async-done | bytes 2097184 | tf_op jit(solution)/shard_map/all_to_all | solution.py:510
  157.2 0.6 slice_bitcast_fusion.after_ref
  157.8 90.2 %all_to_all.21.parts_ref.in_hbm_ref = bf16[32,57,16,128]{3,2,1,0:T(8,128)(2,1)} all-to-all(bf16[32,57,16,128]{3,2,1,0:T(8,128)(2,1)} %shard_map.97), channel_id=1, replica_groups=mesh['seq'=32,'dp'=4] {'seq'}, dimensions={0} | all-to-all | bytes 14942208 | tf_op jit(solution)/shard_map/all_to_all | solution.py:510
  248.0 2.1 shard_map.98.after_ref
  250.1 4.7 %all-to-all-start.3 = ((f32[4,9,8,128]{3,2,1,0:T(8,128)}), f32[4,9,8,128]{3,2,1,0:T(8,128)S(1)}, u32[]{:S(2)}, u32[]{:S(2)}) async-start(f32[4,9,8,128]{3,2,1,0:T(8,128)} %shard_map.98.after_ref), calls=%async_computation.3 | async-start | bytes 294912 | tf_op jit(solution)/shard_map/all_to_all | solution.py:536
  254.8 0.0 copy-start.3
  254.8 0.0 copy-start.4
  254.8 9.5 %shard_map.99 = (bf16[1,32,64,1024]{3,2,1,0:T(8,128)(2,1)}, bf16[1,32,64,1024]{3,2,1,0:T(8,128)(2,1)}) custom-call(bf16[32,16,16,128]{3,2,1,0:T(8,128)(2,1)S(1)} %all-to-all-done.1.lead_hbm, bf16[32,57,16,128]{3,2,1,0:T(8,128)(2,1)} %all_to_all.21.parts_ref.in_hbm_ref, bf16[1,32,64,1024]{3,2,1,0:T(8,128)(2,1)} %cot_hbm.3, ...), custom_call_target="tpu_custom_call" | custom-call | tf_op jit(solution)/shard_map/pallas_call | solution.py:181
  264.3 0.1 all-to-all-done.3.refs_2_
  264.4 0.0 copy-done.3
  264.4 0.0 copy-done.4
  264.4 1.3 shard_map.100
  (1 shorter events, 0.0 us)
Async XLA Ops:
  9.5 106.0 %copy-start = (bf16[1024,1024]{1,0:T(8,128)(2,1)S(1)}, bf16[1024,1024]{1,0:T(8,128)(2,1)}, u32[]{:S(2)}) copy-start(bf16[1024,1024]{1,0:T(8,128)(2,1)} %left_hbm.3) | copy-start | bytes 6291460
  9.6 105.9 %copy-start.1 = (bf16[1024,1024]{1,0:T(8,128)(2,1)S(1)}, bf16[1024,1024]{1,0:T(8,128)(2,1)}, u32[]{:S(2)}) copy-start(bf16[1024,1024]{1,0:T(8,128)(2,1)} %right_hbm.3) | copy-start | bytes 6291460
  9.6 105.9 %copy-start.2 = (s32[8,8]{1,0:T(8,128)S(1)}, s32[8,8]{1,0:T(8,128)}, u32[]{:S(2)}) copy-start(s32[8,8]{1,0:T(8,128)} %refs_1_.1) | copy-start | bytes 772
  122.9 34.3 %all-to-all-start.1 = ((bf16[32,16,16,128]{3,2,1,0:T(8,128)(2,1)}), bf16[32,16,16,128]{3,2,1,0:T(8,128)(2,1)S(1)}, u32[]{:S(2)}, u32[]{:S(2)}) async-start(bf16[32,16,16,128]{3,2,1,0:T(8,128)(2,1)} %get-tuple-element.16), calls=%async_computation.1 | async-start | bytes 4194304 | tf_op jit(solution)/shard_map/all_to_all | solution.py:510
  147.3 2.9 %collective-permute-start = (bf16[32,9,16,128]{3,2,1,0:T(8,128)(2,1)S(1)}, bf16[32,9,16,128]{3,2,1,0:T(8,128)(2,1)S(1)}, u32[]{:S(2)}, u32[]{:S(2)}) collective-permute-start(bf16[32,9,16,128]{3,2,1,0:T(8,128)(2,1)S(1)} %get-tuple-element.20), channel_id=1, source_target_pairs={{0,1},{1,0},{2,3},{3,2},{4,5},{5,4},{6,7},{7,6},{8,9},{9,8},{10,11... | collective-permute-start | bytes 3538952 | tf_op jit(solution)/shard_map/ppermute | solution.py:528
  250.1 14.3 %all-to-all-start.3 = ((f32[4,9,8,128]{3,2,1,0:T(8,128)}), f32[4,9,8,128]{3,2,1,0:T(8,128)S(1)}, u32[]{:S(2)}, u32[]{:S(2)}) async-start(f32[4,9,8,128]{3,2,1,0:T(8,128)} %shard_map.98.after_ref), calls=%async_computation.3 | async-start | bytes 294912 | tf_op jit(solution)/shard_map/all_to_all | solution.py:536
  254.8 9.6 %copy-start.3 = (s32[8,8]{1,0:T(8,128)S(1)}, s32[8,8]{1,0:T(8,128)}, u32[]{:S(2)}) copy-start(s32[8,8]{1,0:T(8,128)} %refs_1_.1) | copy-start | bytes 772
  254.8 9.6 %copy-start.4 = (s32[2]{0:T(128)S(1)}, s32[2]{0:T(128)}, u32[]{:S(2)}) copy-start(s32[2]{0:T(128)} %get-tuple-element.17.place_ref.refs_0_) | copy-start | bytes 28

commit v7 on v6

--- a/solution.py
+++ b/solution.py
@@ -25,6 +25,10 @@
 
 def in_hbm(x):
     return pltpu.with_memory_space_constraint(x, pltpu.HBM)
+
+
+def in_vmem(x):
+    return pltpu.with_memory_space_constraint(x, pltpu.VMEM)
 
 
 def dot(a, b, on_a, on_b):
@@ -444,11 +448,11 @@
     whole = pl.BlockSpec(memory_space=pl.ANY)
     return pl.pallas_call(
         tie_kernel,
-        in_specs=[whole, whole],
+        in_specs=[whole, pl.BlockSpec(memory_space=pltpu.VMEM)],
         out_specs=whole,
         out_shape=pltpu.HBM(parts.shape, BF),
         input_output_aliases={0: 0},
-    )(in_hbm(parts), after)
+    )(in_hbm(parts), in_vmem(after))
 
 
 def fold_kernel(parts_ref, out_ref, got, sem):
@@ -526,7 +530,7 @@
         place, mask_tiles, left_factor, right_factor, parts, first, own
     )
     got = lax.ppermute(give, "dp", [(d, d ^ 1) for d in range(data_count)])
-    parts = swap(tie(add(keep, got, parts), ahead[0, 0]))
+    parts = swap(tie(add(keep, got, parts), ahead))
     sums = fold(parts, mask_tiles.shape[0] + 1, own)
     groups = [
         [at * data_count + d for at in (s, seq_count - 1 - s) for d in (core, core + 2)]

time: 267 us -> 266 us (level)
  no operation moved by 1% of the time
where the time goes in v7:
time: 266 us; the launch traced here: 265 us
  blocking collectives  196 us (74%)
  Pallas kernels  49.9 us (19%)
  starting transfers between devices  9.09 us (3%)
  waiting for transfers between devices  8.63 us (3%)
    all_to_all x2, blocking collectives, swap(): return lax.all_to_all(x, 'seq', split_axis=0, concat_axis=0, tiled=True)  196 us
    pallas_call x1, Pallas kernels, rest(): pl.pallas_call(rest_kernel, in_specs=[smem, smem] + [whole] * 4, out_spec...  20.1 us
    pallas_call x1, Pallas kernels, gather(): pl.pallas_call(gather_kernel, in_specs=[whole] * 5, out_specs=(whole, who...  9.49 us
    pallas_call x1, Pallas kernels, spread(): pl.pallas_call(spread_kernel, in_specs=[smem] + [whole] * 3, out_specs=(p...  8.31 us
    pallas_call x1, Pallas kernels, lead(): pl.pallas_call(lead_kernel, in_specs=[pl.BlockSpec(memory_space=pltpu.SME...  7.44 us
    all_to_all x1, waiting for transfers between devices, swap(): return lax.all_to_all(x, 'seq', split_axis=0, concat_axis=0, tiled=True)  5.7 us
  transfers between devices with their start and end apart: 3, of which 3 were waited for; matrix products, arithmetic and copies ran while one was open for 0% of the time, Pallas kernels for 12%

profile of v7, /device:TPU:0, one launch (start us, length us, event | category | flops | bytes accessed | tf_op | source)
XLA Modules:
  0.0 265.1 jit_solution(18005306466556644356)
XLA Ops:
  0.6 0.6 pad_add_fusion.place_ref
  1.2 8.3 %shard_map.93 = (bf16[32,2,2,32,1024]{4,3,2,1,0:T(8,128)(2,1)S(1)}, s32[2]{0:T(128)}) custom-call(s32[2]{0:T(128)} %pad_add_fusion.place_ref, bf16[1,32,64,1024]{3,2,1,0:T(8,128)(2,1)} %x_hbm.1, bf16[1,32,64,1024]{3,2,1,0:T(8,128)(2,1)} %cot_hbm.3, bf16[1,32,64,1024]{3,2,1,0:T(8,128)(2,1)} %gate_hbm.3), custom_call_target="tpu_custom_call" | custom-call | tf_op jit(solution)/shard_map/pallas_call | solution.py:125
  9.5 0.0 copy-start
  9.6 0.0 copy-start.1
  9.6 0.0 copy-start.2
  9.6 105.9 %all_to_all.20.parts_hbm = bf16[32,2,2,32,1024]{4,3,2,1,0:T(8,128)(2,1)} all-to-all(bf16[32,2,2,32,1024]{4,3,2,1,0:T(8,128)(2,1)S(1)} %get-tuple-element.15), channel_id=1, replica_groups=mesh['seq'=32,'dp'=4] {'seq'}, dimensions={0} | all-to-all | bytes 16777216 | tf_op jit(solution)/shard_map/all_to_all | solution.py:514
  115.5 0.0 copy-done
  115.5 0.0 copy-done.1
  115.5 0.0 copy-done.2
  115.5 7.4 %shard_map.94 = (bf16[32,16,16,128]{3,2,1,0:T(8,128)(2,1)}, bf16[1024,1024]{1,0:T(8,128)(2,1)}) custom-call(s32[8,8]{1,0:T(8,128)S(1)} %copy-done.2, bf16[1024,1024]{1,0:T(8,128)(2,1)S(1)} %copy-done, bf16[1024,1024]{1,0:T(8,128)(2,1)S(1)} %copy-done.1, bf16[32,2,2,32,1024]{4,3,2,1,0:T(8,128)(2,1)} %all_to_all.20.parts_hbm), custom_call_target="tpu_custom_call" | custom-call | tf_op jit(solution)/shard_map/pallas_call | solution.py:280
  122.9 4.3 %all-to-all-start.1 = ((bf16[32,16,16,128]{3,2,1,0:T(8,128)(2,1)}), bf16[32,16,16,128]{3,2,1,0:T(8,128)(2,1)S(1)}, u32[]{:S(2)}, u32[]{:S(2)}) async-start(bf16[32,16,16,128]{3,2,1,0:T(8,128)(2,1)} %get-tuple-element.16), calls=%async_computation.1 | async-start | bytes 4194304 | tf_op jit(solution)/shard_map/all_to_all | solution.py:514
  127.3 20.1 %shard_map.95 = (bf16[32,57,16,128]{3,2,1,0:T(8,128)(2,1)}, f32[32,9,16,128]{3,2,1,0:T(8,128)S(1)}, bf16[32,9,16,128]{3,2,1,0:T(8,128)(2,1)S(1)}) custom-call(s32[2]{0:T(128)} %get-tuple-element.17.place_ref.refs_0_, s32[8,8]{1,0:T(8,128)} %refs_1_.1, bf16[1024,1024]{1,0:T(8,128)(2,1)} %left_hbm.3, bf16[1024,1024]{1,0:T(8,128)(2,1)} %right_hbm.3, ...), custom_call_target="tpu_custom_call" | custom-call | tf_op jit(solution)/shard_map/pallas_call | solution.py:394
  147.3 0.1 collective-permute-start
  147.4 2.8 %collective-permute-done.got_ref = bf16[32,9,16,128]{3,2,1,0:T(8,128)(2,1)S(1)} collective-permute-done((bf16[32,9,16,128]{3,2,1,0:T(8,128)(2,1)S(1)}, bf16[32,9,16,128]{3,2,1,0:T(8,128)(2,1)S(1)}, u32[]{:S(2)}, u32[]{:S(2)}) %collective-permute-start) | collective-permute-done | bytes 1179680 | tf_op jit(solution)/shard_map/ppermute | solution.py:532
  150.3 1.2 shard_map.96.parts_ref
  151.5 5.7 %all-to-all-done.1.after_ref.lead_hbm = bf16[32,16,16,128]{3,2,1,0:T(8,128)(2,1)S(1)} async-done(((bf16[32,16,16,128]{3,2,1,0:T(8,128)(2,1)}), bf16[32,16,16,128]{3,2,1,0:T(8,128)(2,1)S(1)}, u32[]{:S(2)}, u32[]{:S(2)}) %all-to-all-start.1) | async-done | bytes 2097184 | tf_op jit(solution)/shard_map/all_to_all | solution.py:514
  157.2 90.2 %all_to_all.21.parts_ref.in_hbm_ref = bf16[32,57,16,128]{3,2,1,0:T(8,128)(2,1)} all-to-all(bf16[32,57,16,128]{3,2,1,0:T(8,128)(2,1)} %shard_map.97), channel_id=1, replica_groups=mesh['seq'=32,'dp'=4] {'seq'}, dimensions={0} | all-to-all | bytes 14942208 | tf_op jit(solution)/shard_map/all_to_all | solution.py:514
  247.4 2.1 shard_map.98.after_ref
  249.5 4.7 %all-to-all-start.3 = ((f32[4,9,8,128]{3,2,1,0:T(8,128)}), f32[4,9,8,128]{3,2,1,0:T(8,128)S(1)}, u32[]{:S(2)}, u32[]{:S(2)}) async-start(f32[4,9,8,128]{3,2,1,0:T(8,128)} %shard_map.98.after_ref), calls=%async_computation.3 | async-start | bytes 294912 | tf_op jit(solution)/shard_map/all_to_all | solution.py:540
  254.2 0.0 copy-start.3
  254.2 0.0 copy-start.4
  254.2 9.5 %shard_map.99 = (bf16[1,32,64,1024]{3,2,1,0:T(8,128)(2,1)}, bf16[1,32,64,1024]{3,2,1,0:T(8,128)(2,1)}) custom-call(bf16[32,16,16,128]{3,2,1,0:T(8,128)(2,1)S(1)} %all-to-all-done.1.after_ref.lead_hbm, bf16[32,57,16,128]{3,2,1,0:T(8,128)(2,1)} %all_to_all.21.parts_ref.in_hbm_ref, bf16[1,32,64,1024]{3,2,1,0:T(8,128)(2,1)} %cot_hbm.3, ...), custom_call_target="tpu_custom_call" | custom-call | tf_op jit(solution)/shard_map/pallas_call | solution.py:185
  263.7 0.1 all-to-all-done.3.refs_2_
  263.8 0.0 copy-done.3
  263.8 0.0 copy-done.4
  263.8 1.3 shard_map.100
  (1 shorter events, 0.0 us)
Async XLA Ops:
  9.5 106.0 %copy-start = (bf16[1024,1024]{1,0:T(8,128)(2,1)S(1)}, bf16[1024,1024]{1,0:T(8,128)(2,1)}, u32[]{:S(2)}) copy-start(bf16[1024,1024]{1,0:T(8,128)(2,1)} %left_hbm.3) | copy-start | bytes 6291460
  9.6 105.9 %copy-start.1 = (bf16[1024,1024]{1,0:T(8,128)(2,1)S(1)}, bf16[1024,1024]{1,0:T(8,128)(2,1)}, u32[]{:S(2)}) copy-start(bf16[1024,1024]{1,0:T(8,128)(2,1)} %right_hbm.3) | copy-start | bytes 6291460
  9.6 105.9 %copy-start.2 = (s32[8,8]{1,0:T(8,128)S(1)}, s32[8,8]{1,0:T(8,128)}, u32[]{:S(2)}) copy-start(s32[8,8]{1,0:T(8,128)} %refs_1_.1) | copy-start | bytes 772
  122.9 34.3 %all-to-all-start.1 = ((bf16[32,16,16,128]{3,2,1,0:T(8,128)(2,1)}), bf16[32,16,16,128]{3,2,1,0:T(8,128)(2,1)S(1)}, u32[]{:S(2)}, u32[]{:S(2)}) async-start(bf16[32,16,16,128]{3,2,1,0:T(8,128)(2,1)} %get-tuple-element.16), calls=%async_computation.1 | async-start | bytes 4194304 | tf_op jit(solution)/shard_map/all_to_all | solution.py:514
  147.3 2.9 %collective-permute-start = (bf16[32,9,16,128]{3,2,1,0:T(8,128)(2,1)S(1)}, bf16[32,9,16,128]{3,2,1,0:T(8,128)(2,1)S(1)}, u32[]{:S(2)}, u32[]{:S(2)}) collective-permute-start(bf16[32,9,16,128]{3,2,1,0:T(8,128)(2,1)S(1)} %get-tuple-element.20), channel_id=1, source_target_pairs={{0,1},{1,0},{2,3},{3,2},{4,5},{5,4},{6,7},{7,6},{8,9},{9,8},{10,11... | collective-permute-start | bytes 3538952 | tf_op jit(solution)/shard_map/ppermute | solution.py:532
  249.5 14.3 %all-to-all-start.3 = ((f32[4,9,8,128]{3,2,1,0:T(8,128)}), f32[4,9,8,128]{3,2,1,0:T(8,128)S(1)}, u32[]{:S(2)}, u32[]{:S(2)}) async-start(f32[4,9,8,128]{3,2,1,0:T(8,128)} %shard_map.98.after_ref), calls=%async_computation.3 | async-start | bytes 294912 | tf_op jit(solution)/shard_map/all_to_all | solution.py:540
  254.2 9.6 %copy-start.3 = (s32[8,8]{1,0:T(8,128)S(1)}, s32[8,8]{1,0:T(8,128)}, u32[]{:S(2)}) copy-start(s32[8,8]{1,0:T(8,128)} %refs_1_.1) | copy-start | bytes 772
  254.2 9.6 %copy-start.4 = (s32[2]{0:T(128)S(1)}, s32[2]{0:T(128)}, u32[]{:S(2)}) copy-start(s32[2]{0:T(128)} %get-tuple-element.17.place_ref.refs_0_) | copy-start | bytes 28
